TPU v7x, 512 devices: a whole 4x8x8 slice. The times are simulated.
512 devices in a mesh: gx: 2 (over core), gy: 2 (over x_lo), gz: 128 (over z, y, x_hi).
Axes of the slice: x: 4 (x_hi: 2, x_lo: 2; x = x_hi * 2 + x_lo), y: 8, z: 8, core: 2. Of those that a mesh axis runs over, the one named last changes fastest.
Arguments:
- populations: bfloat16 [7, 4, 2, 128, 32768], P(None, 'gx', 'gy', 'gz'), may hold values from 0 to 0.25
- adjoint_final: bfloat16 [7, 4, 2, 128, 32768], P(None, 'gx', 'gy', 'gz'), may hold values from -6 to 6
- velocity: bfloat16 [3, 4, 2, 128, 32768], P(None, 'gx', 'gy', 'gz'), may hold values from -0.14941406 to 0.14941406
- particle_kappa: float32 [4, 2, 128, 32768], P('gx', 'gy', 'gz'), may hold values from 0.02 to 0.3
- solid_label: int32 [4, 2, 128, 32768], P('gx', 'gy', 'gz'), may hold values 0 or 1
- tile_active: int32 [4, 2, 128], P('gx', 'gy', 'gz'), may hold values 0 or 1
Outputs:
- adjoint_first: float32 [7, 4, 2, 128, 32768], P(None, 'gx', 'gy', 'gz')
- kappa_gradient: float32 [4, 2, 128, 32768], P('gx', 'gy', 'gz')
All inputs are finite; a program needn't handle non-finite values. No bound on the sum of `solid_label` or of `tile_active` on one device may be relied on, other than what follows from the above.
Results may differ from a plain program's by a relative error of at most 0.00045.
Values sent between devices are 32-bit elements; how exact they have to be, the bound alone decides.
A program may use at most 64 MiB of HBM per device.

v0:
```python
import jax
import jax.numpy as jnp
from jax import lax
from jax.sharding import PartitionSpec as P

EDGE = 32


DIRECTIONS = ((0, 0), (0, 1), (0, -1), (1, 1), (1, -1), (2, 1), (2, -1))
FLUID_KAPPA = 1.0 / 6.0


def passed_along(array, axis, by):
    count = lax.axis_size(axis)
    pairs = [(i, i + by) for i in range(count) if 0 <= i + by < count]
    return lax.ppermute(array, axis, pairs)


def to_local(block):
    return block.reshape((block.shape[0], block.shape[1] * EDGE, EDGE * EDGE))


def factor(number, drift):
    if number == 0:
        return 0.25
    dim, sign = DIRECTIONS[number]
    return 0.125 * (1.0 + 4.0 * sign * drift[dim])


def selector(offset):
    lanes = lax.broadcasted_iota(jnp.int32, (EDGE * EDGE, EDGE), 0)
    column = lax.broadcasted_iota(jnp.int32, (EDGE * EDGE, EDGE), 1)
    return jnp.where(lanes == column * EDGE + offset, 1.0, 0.0).astype(jnp.float32)


def take_face(field, dim, first):
    if dim == 0:
        return field[0:1] if first else field[-1:]
    if dim == 1:
        return field[:, :EDGE] if first else field[:, -EDGE:]
    picker = selector(0 if first else EDGE - 1)
    return jnp.dot(
        field, picker, precision=lax.Precision.HIGHEST, preferred_element_type=jnp.float32
    )


def place_face(field, face, dim, forward):
    rows, lanes = field.shape
    zero = jnp.zeros((), field.dtype)
    if dim == 0:
        if forward:
            return lax.pad(field, zero, ((1, -1, 0), (0, 0, 0))) + lax.pad(
                face, zero, ((0, rows - 1, 0), (0, 0, 0))
            )
        return lax.pad(field, zero, ((-1, 1, 0), (0, 0, 0))) + lax.pad(
            face, zero, ((rows - 1, 0, 0), (0, 0, 0))
        )
    if dim == 1:
        if forward:
            return lax.pad(field, zero, ((0, 0, 0), (EDGE, -EDGE, 0))) + lax.pad(
                face, zero, ((0, 0, 0), (0, lanes - EDGE, 0))
            )
        return lax.pad(field, zero, ((0, 0, 0), (-EDGE, EDGE, 0))) + lax.pad(
            face, zero, ((0, 0, 0), (lanes - EDGE, 0, 0))
        )
    lane_pos = lax.broadcasted_iota(jnp.int32, field.shape, 1) % EDGE
    if forward:
        inner = lax.pad(field, zero, ((0, 0, 0), (1, -1, 0)))
        spread = jnp.dot(
            face, selector(0).T, precision=lax.Precision.HIGHEST, preferred_element_type=jnp.float32
        )
        return jnp.where(lane_pos == 0, 0.0, inner) + spread
    inner = lax.pad(field, zero, ((0, 0, 0), (-1, 1, 0)))
    spread = jnp.dot(
        face,
        selector(EDGE - 1).T,
        precision=lax.Precision.HIGHEST,
        preferred_element_type=jnp.float32,
    )
    return jnp.where(lane_pos == EDGE - 1, 0.0, inner) + spread


def send_faces(faces, dim, forward):
    if dim == 0:
        if forward:
            return passed_along(faces, "gx", 1)
        return passed_along(faces, "gx", -1)
    if dim == 1:
        if forward:
            return passed_along(faces, "gy", 1)
        return passed_along(faces, "gy", -1)
    if forward:
        return passed_along(faces, "gz", 1)
    return passed_along(faces, "gz", -1)


def stream_many(fields, flips):
    results = [[field[0], None, None, None, None, None, None] for field in fields]
    for dim in range(3):
        for forward in (True, False):
            chosen = []
            which = 0
            for number in range(1, 7):
                axis_dim, sign = DIRECTIONS[number]
                if axis_dim == dim and (sign * flips[which] > 0) == forward:
                    chosen.append((which, number))
            faces = jnp.stack(
                [take_face(fields[which][number], dim, not forward) for which, number in chosen]
            )
            arrived = send_faces(faces, dim, forward)
            for position, (which, number) in enumerate(chosen):
                results[which][number] = place_face(
                    fields[which][number], arrived[position], dim, forward
                )
    return results


def adjoint_step(pulled, state, relax_rate, drift, active):
    weighted = factor(0, drift) * pulled[0]
    for number in range(1, 7):
        weighted = weighted + factor(number, drift) * pulled[number]
    adjoint_prev = [
        active * ((1.0 - relax_rate) * pulled[number] + relax_rate * weighted)
        for number in range(7)
    ]
    state_total = state[0]
    product_total = pulled[0] * state[0]
    for number in range(1, 7):
        state_total = state_total + state[number]
        product_total = product_total + pulled[number] * state[number]
    term = active * (weighted * state_total - product_total)
    return (adjoint_prev, term)


def on_device(populations, adjoint_final, velocity, particle_kappa, solid_label, tile_active):
    tiles_here = populations.shape[1]
    active = jnp.repeat(tile_active.reshape(tiles_here).astype(jnp.float32), EDGE)[:, None]
    solid = to_local(solid_label[None])[0].astype(jnp.float32)
    kappa = jnp.where(solid > 0.5, to_local(particle_kappa[None])[0], FLUID_KAPPA)
    relax_rate = 1.0 / (4.0 * kappa + 0.5)
    drift = to_local(velocity).astype(jnp.float32) * (1.0 - solid)
    first_block = to_local(populations).astype(jnp.float32)
    state_first = [first_block[number] for number in range(7)]
    total_first = state_first[0]
    for number in range(1, 7):
        total_first = total_first + state_first[number]
    post = [
        active
        * (
            state_first[number]
            - relax_rate * (state_first[number] - factor(number, drift) * total_first)
        )
        for number in range(7)
    ]
    final_block = to_local(adjoint_final).astype(jnp.float32)
    final_local = [final_block[number] for number in range(7)]
    state_second = stream_many([post], [1])[0]
    pulled_final = stream_many([final_local], [-1])[0]
    adjoint_middle, term_second = adjoint_step(
        pulled_final, state_second, relax_rate, drift, active
    )
    pulled_middle = stream_many([adjoint_middle], [-1])[0]
    adjoint_first, term_first = adjoint_step(pulled_middle, state_first, relax_rate, drift, active)
    gradient = solid * (-4.0 * relax_rate * relax_rate) * (term_second + term_first)
    voxels = EDGE * EDGE * EDGE
    return (
        jnp.stack(adjoint_first).reshape((7, tiles_here, 1, 1, voxels)),
        gradient.reshape((tiles_here, 1, 1, voxels)),
    )


def solution(mesh):
    placed = (
        P(None, "gx", "gy", "gz", None),
        P(None, "gx", "gy", "gz", None),
        P(None, "gx", "gy", "gz", None),
        P("gx", "gy", "gz", None),
        P("gx", "gy", "gz", None),
        P("gx", "gy", "gz"),
    )
    return jax.shard_map(
        on_device,
        mesh=mesh,
        in_specs=placed,
        out_specs=(P(None, "gx", "gy", "gz", None), P("gx", "gy", "gz", None)),
        check_vma=False,
    )
```

profile of v0, /device:TPU:255, one launch (start us, length us, event | category | flops | bytes accessed | tf_op | source)
XLA Modules:
  0.0 121.4 jit_solution(12287439201571520990)
XLA Ops:
  3.0 3.0 %collective-permute-start.4 = (f32[1,64,32]{1,2,0:T(8,128)}, f32[1,64,32]{1,2,0:T(8,128)}, u32[]{:S(2)}, u32[]{:S(2)}) collective-permute-start(f32[1,64,32]{1,2,0:T(8,128)} %fusion.54), channel_id=1, source_target_pairs={{1,0},{2,1},{3,2},{4,3},{5,4},{6,5},{7,6},{8,7},{9,8},{10,9},{11,1... | collective-permute-start | bytes 24584 | tf_op jit(solution)/shard_map/ppermute | solution.py:16
  9.4 4.7 %collective-permute-start.2 = (f32[1,64,32]{2,1,0:T(8,128)S(1)}, f32[1,64,32]{2,1,0:T(8,128)}, u32[]{:S(2)}, u32[]{:S(2)}) collective-permute-start(f32[1,64,32]{2,1,0:T(8,128)S(1)} %slice_bitcast_fusion.5), channel_id=1, source_target_pairs={{128,0},{129,1},{130,2},{131,3},{132,4},{133,5},{134,6},{135,7},{1... | collective-permute-start | bytes 24584 | tf_op jit(solution)/shard_map/ppermute | solution.py:16
  15.2 8.0 %collective-permute-start.5 = (f32[1,64,32]{1,2,0:T(8,128)}, f32[1,64,32]{1,2,0:T(8,128)}, u32[]{:S(2)}, u32[]{:S(2)}) collective-permute-start(f32[1,64,32]{1,2,0:T(8,128)} %fusion.57), channel_id=1, source_target_pairs={{0,1},{1,2},{2,3},{3,4},{4,5},{5,6},{6,7},{7,8},{8,9},{9,10},{10,1... | collective-permute-start | bytes 24584 | tf_op jit(solution)/shard_map/ppermute | solution.py:16
  23.2 1.7 %convert_element_type.39 = f32[7,64,1024]{2,1,0:T(8,128)} reshape(bf16[7,2,1,1,32768]{4,1,3,2,0:T(2,128)(2,1)S(1)} %copy-done) | data formatting | bytes 2752512 | tf_op jit(solution)/shard_map/convert_element_type | solution.py:155
  26.2 4.3 %collective-permute-start = (f32[1,1,1024]{2,1,0:T(1,128)}, f32[1,1,1024]{2,1,0:T(1,128)}, u32[]{:S(2)}, u32[]{:S(2)}) collective-permute-start(f32[1,1,1024]{2,1,0:T(1,128)} %get-tuple-element.11), channel_id=1, source_target_pairs={{256,0},{257,1},{258,2},{259,3},{260,4},{261,5},{262,6},{263,7},{2... | collective-permute-start | bytes 12296 | tf_op jit(solution)/shard_map/ppermute | solution.py:16
  46.6 1.9 %squeeze.127 = f32[64,1024]{1,0:T(8,128)} reshape(f32[1,2,1,1,32768]{4,1,3,2,0:T(2,128)} %get-tuple-element.22) | data formatting | bytes 524288 | tf_op jit(solution)/shard_map/squeeze | solution.py:156
  48.5 1.9 %squeeze.118 = f32[64,1024]{1,0:T(8,128)} reshape(f32[1,2,1,1,32768]{4,1,3,2,0:T(2,128)} %get-tuple-element.18) | data formatting | bytes 524288 | tf_op jit(solution)/shard_map/squeeze | solution.py:156
  50.4 1.9 %squeeze.119 = f32[64,1024]{1,0:T(8,128)} reshape(f32[1,2,1,1,32768]{4,1,3,2,0:T(2,128)} %get-tuple-element.20) | data formatting | bytes 524288 | tf_op jit(solution)/shard_map/squeeze | solution.py:156
  52.2 1.9 %squeeze.121 = f32[64,1024]{1,0:T(8,128)} reshape(f32[1,2,1,1,32768]{4,1,3,2,0:T(2,128)} %get-tuple-element.21) | data formatting | bytes 524288 | tf_op jit(solution)/shard_map/squeeze | solution.py:156
  56.3 1.7 %fusion.33 = f32[64,1024]{1,0:T(8,128)S(1)} fusion(f32[64,1024]{1,0:T(8,128)} %squeeze.127, s32[32]{0:T(128)} %copy-done.48, s32[1024]{0:T(1024)} %get-tuple-element.47, s32[1024]{0:T(1024)} %get-tuple-element.48, pred[1024]{0:T(1024)(128)(4,1)} %fusion.165, f32[1,64,32]{1,2,0:T(8,128)} %collective-permute-done.4), kind=kOutput, calls=%fused_computation.27 | convolution fusion | flops 25493504 | bytes 541824 | tf_op jit(solution)/shard_map/dot_general | solution.py:74
  58.0 2.1 %collective-permute-start.16 = (f32[1,64,32]{1,2,0:T(8,128)}, f32[1,64,32]{1,2,0:T(8,128)S(1)}, u32[]{:S(2)}, u32[]{:S(2)}) collective-permute-start(f32[1,64,32]{1,2,0:T(8,128)} %fusion.51), channel_id=1, source_target_pairs={{0,1},{1,2},{2,3},{3,4},{4,5},{5,6},{6,7},{7,8},{8,9},{9,10},{10,1... | collective-permute-start | bytes 24584 | tf_op jit(solution)/shard_map/ppermute | solution.py:16
  60.2 2.4 %add_multiply_fusion.10 = (f32[64,1024]{1,0:T(8,128)S(1)}, f32[64,1024]{1,0:T(8,128)S(1)}, f32[64,1024]{1,0:T(8,128)S(1)}) fusion(f32[64,1024]{1,0:T(8,128)S(1)} %get-tuple-element.6, f32[64]{0:T(128)} %copy-done.35, f32[64,32]{1,0:T(8,128)} %bitcast.7, f32[64,1024]{1,0:T(8,128)} %copy-done.21, f32[64,1024]{1,0:T(8,128)S(1)} %fusion.33, ...), kind=kOutput, calls=%fused_computation.145 | convolution fusion | flops 28180480 | bytes 3712384 | tf_op jit(solution)/shard_map/dot_general | solution.py:69
  64.5 4.9 %collective-permute-start.10 = (f32[1,64,32]{1,2,0:T(8,128)S(1)}, f32[1,64,32]{1,2,0:T(8,128)S(1)}, u32[]{:S(2)}, u32[]{:S(2)}) collective-permute-start(f32[1,64,32]{1,2,0:T(8,128)S(1)} %fusion.42), channel_id=1, source_target_pairs={{1,0},{2,1},{3,2},{4,3},{5,4},{6,5},{7,6},{8,7},{9,8},{10,9},{11,1... | collective-permute-start | bytes 24584 | tf_op jit(solution)/shard_map/ppermute | solution.py:16
  71.3 6.1 %collective-permute-start.11 = (f32[1,64,32]{1,2,0:T(8,128)S(1)}, f32[1,64,32]{1,2,0:T(8,128)S(1)}, u32[]{:S(2)}, u32[]{:S(2)}) collective-permute-start(f32[1,64,32]{1,2,0:T(8,128)S(1)} %fusion.48), channel_id=1, source_target_pairs={{0,1},{1,2},{2,3},{3,4},{4,5},{5,6},{6,7},{7,8},{8,9},{9,10},{10,1... | collective-permute-start | bytes 24584 | tf_op jit(solution)/shard_map/ppermute | solution.py:16
  77.5 3.6 %collective-permute-start.6 = (f32[1,1,1024]{2,1,0:T(1,128)S(1)}, f32[1,1,1024]{2,1,0:T(1,128)S(1)}, u32[]{:S(2)}, u32[]{:S(2)}) collective-permute-start(f32[1,1,1024]{2,1,0:T(1,128)S(1)} %slice_bitcast_fusion.9), channel_id=1, source_target_pairs={{256,0},{257,1},{258,2},{259,3},{260,4},{261,5},{262,6},{263,7},{2... | collective-permute-start | bytes 12296 | tf_op jit(solution)/shard_map/ppermute | solution.py:16
  83.2 3.7 %collective-permute-start.8 = (f32[1,64,32]{2,1,0:T(8,128)S(1)}, f32[1,64,32]{2,1,0:T(8,128)S(1)}, u32[]{:S(2)}, u32[]{:S(2)}) collective-permute-start(f32[1,64,32]{2,1,0:T(8,128)S(1)} %slice_bitcast_fusion.3), channel_id=1, source_target_pairs={{128,0},{129,1},{130,2},{131,3},{132,4},{133,5},{134,6},{135,7},{1... | collective-permute-start | bytes 24584 | tf_op jit(solution)/shard_map/ppermute | solution.py:16
  88.9 4.0 %collective-permute-start.15 = (f32[1,64,32]{2,1,0:T(8,128)S(1)}, f32[1,64,32]{2,1,0:T(8,128)S(1)}, u32[]{:S(2)}, u32[]{:S(2)}) collective-permute-start(f32[1,64,32]{2,1,0:T(8,128)S(1)} %slice_bitcast_fusion), channel_id=1, source_target_pairs={{128,0},{129,1},{130,2},{131,3},{132,4},{133,5},{134,6},{135,7},{1... | collective-permute-start | bytes 24584 | tf_op jit(solution)/shard_map/ppermute | solution.py:16
  92.9 3.9 %collective-permute-start.13 = (f32[1,1,1024]{2,1,0:T(1,128)S(1)}, f32[1,1,1024]{2,1,0:T(1,128)S(1)}, u32[]{:S(2)}, u32[]{:S(2)}) collective-permute-start(f32[1,1,1024]{2,1,0:T(1,128)S(1)} %copy-done.41), channel_id=1, source_target_pairs={{256,0},{257,1},{258,2},{259,3},{260,4},{261,5},{262,6},{263,7},{2... | collective-permute-start | bytes 12296 | tf_op jit(solution)/shard_map/ppermute | solution.py:16
  96.8 2.1 %collective-permute-start.17 = (f32[1,64,32]{1,2,0:T(8,128)S(1)}, f32[1,64,32]{1,2,0:T(8,128)S(1)}, u32[]{:S(2)}, u32[]{:S(2)}) collective-permute-start(f32[1,64,32]{1,2,0:T(8,128)S(1)} %fusion.45), channel_id=1, source_target_pairs={{1,0},{2,1},{3,2},{4,3},{5,4},{6,5},{7,6},{8,7},{9,8},{10,9},{11,1... | collective-permute-start | bytes 24584 | tf_op jit(solution)/shard_map/ppermute | solution.py:16
  100.4 1.8 %add_multiply_fusion = (f32[64,1024]{1,0:T(8,128)}, f32[64,1024]{1,0:T(8,128)}, f32[64,1024]{1,0:T(8,128)S(1)}) fusion(f32[64,1024]{1,0:T(8,128)S(1)} %get-tuple-element.6, f32[64]{0:T(128)S(1)} %copy-done.36, f32[64,1024]{1,0:T(8,128)S(1)} %fusion.36, f32[3,64,1024]{2,1,0:T(8,128)S(1)} %broadcast_multiply_fusion, f32[64,32]{1,0:T(8,128)S(1)} %bitcast.269, ...), kind=kOutput, calls=%fused_computation.135 | convolution fusion | flops 28377088 | bytes 3974528 | tf_op jit(solution)/shard_map/dot_general | solution.py:69
  102.2 5.0 %collective-permute-done.17 = f32[1,64,32]{1,2,0:T(8,128)S(1)} collective-permute-done((f32[1,64,32]{1,2,0:T(8,128)S(1)}, f32[1,64,32]{1,2,0:T(8,128)S(1)}, u32[]{:S(2)}, u32[]{:S(2)}) %collective-permute-start.17) | collective-permute-done | bytes 8224 | tf_op jit(solution)/shard_map/ppermute | solution.py:16
  107.3 3.2 %fusion.79 = f32[64,1024]{1,0:T(8,128)} fusion(f32[64,1024]{1,0:T(8,128)S(1)} %convert_element_type.35, f32[64,1024]{1,0:T(8,128)S(1)} %get-tuple-element.6, f32[64,1024]{1,0:T(8,128)S(1)} %get-tuple-element.46, f32[64,1024]{1,0:T(8,128)S(1)} %squeeze.145, f32[64,1024]{1,0:T(8,128)S(1)} %fusion.36, f32[64,1024]{1,0:T(8,128)S(1)} %squeeze.144, ...), kind=kOutput, calls=%fused_computation.79 | convolution fusion | flops 31719424 | bytes 9004416 | tf_op jit(solution)/shard_map/dot_general | solution.py:74
  110.5 2.0 %reshape.113 = f32[2,1,1,32768]{3,2,1,0:T(1,128)} reshape(f32[64,1024]{1,0:T(8,128)} %fusion.79) | data formatting | bytes 524288 | tf_op jit(solution)/shard_map/reshape | solution.py:168
  112.4 1.7 %add_multiply_fusion.1 = (f32[64,1024]{1,0:T(8,128)S(1)}, f32[64,1024]{1,0:T(8,128)S(1)}, f32[64,1024]{1,0:T(8,128)S(1)}, f32[64,1024]{1,0:T(8,128)S(1)}, f32[64,1024]{1,0:T(8,128)S(1)}, /*index=5*/f32[64,1024]{1,0:T(8,128)S(1)}) fusion(f32[64,1024]{1,0:T(8,128)} %get-tuple-element.8, f32[64,1024]{1,0:T(8,128)} %copy-done.28, ...), kind=kLoop, calls=%fused_computation.136 | loop fusion | flops 1769472 | bytes 3956992 | tf_op jit(solution)/shard_map/mul | solution.py:123
  (188 shorter events, 42.5 us)
Async XLA Ops:
  0.7 41.6 %copy-start.44 = (s32[32]{0:T(128)}, s32[32]{0:T(128)S(1)}, u32[]{:S(2)}) copy-start(s32[32]{0:T(128)S(1)} %iota_multiply_fusion) | copy-start | bytes 388
  3.0 52.1 %collective-permute-start.4 = (f32[1,64,32]{1,2,0:T(8,128)}, f32[1,64,32]{1,2,0:T(8,128)}, u32[]{:S(2)}, u32[]{:S(2)}) collective-permute-start(f32[1,64,32]{1,2,0:T(8,128)} %fusion.54), channel_id=1, source_target_pairs={{1,0},{2,1},{3,2},{4,3},{5,4},{6,5},{7,6},{8,7},{9,8},{10,9},{11,1... | collective-permute-start | bytes 24584 | tf_op jit(solution)/shard_map/ppermute | solution.py:16
  7.8 52.3 %collective-permute-start.3 = (f32[1,64,32]{2,1,0:T(8,128)S(1)}, f32[1,64,32]{2,1,0:T(8,128)S(1)}, u32[]{:S(2)}, u32[]{:S(2)}) collective-permute-start(f32[1,64,32]{2,1,0:T(8,128)S(1)} %slice_bitcast_fusion.4), channel_id=1, source_target_pairs={{0,128},{1,129},{2,130},{3,131},{4,132},{5,133},{6,134},{7,135},{8... | collective-permute-start | bytes 24584 | tf_op jit(solution)/shard_map/ppermute | solution.py:16
  9.4 50.8 %collective-permute-start.2 = (f32[1,64,32]{2,1,0:T(8,128)S(1)}, f32[1,64,32]{2,1,0:T(8,128)}, u32[]{:S(2)}, u32[]{:S(2)}) collective-permute-start(f32[1,64,32]{2,1,0:T(8,128)S(1)} %slice_bitcast_fusion.5), channel_id=1, source_target_pairs={{128,0},{129,1},{130,2},{131,3},{132,4},{133,5},{134,6},{135,7},{1... | collective-permute-start | bytes 24584 | tf_op jit(solution)/shard_map/ppermute | solution.py:16
  15.2 45.0 %collective-permute-start.5 = (f32[1,64,32]{1,2,0:T(8,128)}, f32[1,64,32]{1,2,0:T(8,128)}, u32[]{:S(2)}, u32[]{:S(2)}) collective-permute-start(f32[1,64,32]{1,2,0:T(8,128)} %fusion.57), channel_id=1, source_target_pairs={{0,1},{1,2},{2,3},{3,4},{4,5},{5,6},{6,7},{7,8},{8,9},{9,10},{10,1... | collective-permute-start | bytes 24584 | tf_op jit(solution)/shard_map/ppermute | solution.py:16
  26.2 31.8 %collective-permute-start = (f32[1,1,1024]{2,1,0:T(1,128)}, f32[1,1,1024]{2,1,0:T(1,128)}, u32[]{:S(2)}, u32[]{:S(2)}) collective-permute-start(f32[1,1,1024]{2,1,0:T(1,128)} %get-tuple-element.11), channel_id=1, source_target_pairs={{256,0},{257,1},{258,2},{259,3},{260,4},{261,5},{262,6},{263,7},{2... | collective-permute-start | bytes 12296 | tf_op jit(solution)/shard_map/ppermute | solution.py:16
  55.0 5.1 %collective-permute-start.1 = (f32[1,1,1024]{2,1,0:T(1,128)}, f32[1,1,1024]{2,1,0:T(1,128)S(1)}, u32[]{:S(2)}, u32[]{:S(2)}) collective-permute-start(f32[1,1,1024]{2,1,0:T(1,128)} %get-tuple-element.12), channel_id=1, source_target_pairs={{0,256},{1,257},{2,258},{3,259},{4,260},{5,261},{6,262},{7,263},{8... | collective-permute-start | bytes 12296 | tf_op jit(solution)/shard_map/ppermute | solution.py:16
  58.0 23.1 %collective-permute-start.16 = (f32[1,64,32]{1,2,0:T(8,128)}, f32[1,64,32]{1,2,0:T(8,128)S(1)}, u32[]{:S(2)}, u32[]{:S(2)}) collective-permute-start(f32[1,64,32]{1,2,0:T(8,128)} %fusion.51), channel_id=1, source_target_pairs={{0,1},{1,2},{2,3},{3,4},{4,5},{5,6},{6,7},{7,8},{8,9},{9,10},{10,1... | collective-permute-start | bytes 24584 | tf_op jit(solution)/shard_map/ppermute | solution.py:16
  62.6 44.6 %copy-start.13 = (f32[64,1024]{1,0:T(8,128)}, f32[64,1024]{1,0:T(8,128)S(1)}, u32[]{:S(2)}) copy-start(f32[64,1024]{1,0:T(8,128)S(1)} %get-tuple-element.10) | copy-start | bytes 786436
  62.6 44.5 %copy-start.20 = (f32[64,1024]{1,0:T(8,128)}, f32[64,1024]{1,0:T(8,128)S(1)}, u32[]{:S(2)}) copy-start(f32[64,1024]{1,0:T(8,128)S(1)} %get-tuple-element.9) | copy-start | bytes 786436
  63.9 43.3 %copy-start.4 = (f32[64,1024]{1,0:T(8,128)}, f32[64,1024]{1,0:T(8,128)S(1)}, u32[]{:S(2)}) copy-start(f32[64,1024]{1,0:T(8,128)S(1)} %get-tuple-element.40) | copy-start | bytes 786436
  63.9 43.3 %copy-start.5 = (f32[64,1024]{1,0:T(8,128)}, f32[64,1024]{1,0:T(8,128)S(1)}, u32[]{:S(2)}) copy-start(f32[64,1024]{1,0:T(8,128)S(1)} %get-tuple-element.41) | copy-start | bytes 786436
  63.9 36.4 %copy-start.11 = (f32[64,1024]{1,0:T(8,128)S(1)}, f32[64,1024]{1,0:T(8,128)}, u32[]{:S(2)}) copy-start(f32[64,1024]{1,0:T(8,128)} %squeeze.118) | copy-start | bytes 786436
  64.5 18.7 %collective-permute-start.10 = (f32[1,64,32]{1,2,0:T(8,128)S(1)}, f32[1,64,32]{1,2,0:T(8,128)S(1)}, u32[]{:S(2)}, u32[]{:S(2)}) collective-permute-start(f32[1,64,32]{1,2,0:T(8,128)S(1)} %fusion.42), channel_id=1, source_target_pairs={{1,0},{2,1},{3,2},{4,3},{5,4},{6,5},{7,6},{8,7},{9,8},{10,9},{11,1... | collective-permute-start | bytes 24584 | tf_op jit(solution)/shard_map/ppermute | solution.py:16
  69.5 23.5 %collective-permute-start.9 = (f32[1,64,32]{2,1,0:T(8,128)S(1)}, f32[1,64,32]{2,1,0:T(8,128)S(1)}, u32[]{:S(2)}, u32[]{:S(2)}) collective-permute-start(f32[1,64,32]{2,1,0:T(8,128)S(1)} %slice_bitcast_fusion.2), channel_id=1, source_target_pairs={{0,128},{1,129},{2,130},{3,131},{4,132},{5,133},{6,134},{7,135},{8... | collective-permute-start | bytes 24584 | tf_op jit(solution)/shard_map/ppermute | solution.py:16
  71.3 25.5 %collective-permute-start.11 = (f32[1,64,32]{1,2,0:T(8,128)S(1)}, f32[1,64,32]{1,2,0:T(8,128)S(1)}, u32[]{:S(2)}, u32[]{:S(2)}) collective-permute-start(f32[1,64,32]{1,2,0:T(8,128)S(1)} %fusion.48), channel_id=1, source_target_pairs={{0,1},{1,2},{2,3},{3,4},{4,5},{5,6},{6,7},{7,8},{8,9},{9,10},{10,1... | collective-permute-start | bytes 24584 | tf_op jit(solution)/shard_map/ppermute | solution.py:16
  77.5 10.1 %collective-permute-start.6 = (f32[1,1,1024]{2,1,0:T(1,128)S(1)}, f32[1,1,1024]{2,1,0:T(1,128)S(1)}, u32[]{:S(2)}, u32[]{:S(2)}) collective-permute-start(f32[1,1,1024]{2,1,0:T(1,128)S(1)} %slice_bitcast_fusion.9), channel_id=1, source_target_pairs={{256,0},{257,1},{258,2},{259,3},{260,4},{261,5},{262,6},{263,7},{2... | collective-permute-start | bytes 12296 | tf_op jit(solution)/shard_map/ppermute | solution.py:16
  81.1 7.8 %collective-permute-start.7 = (f32[1,1,1024]{2,1,0:T(1,128)S(1)}, f32[1,1,1024]{2,1,0:T(1,128)S(1)}, u32[]{:S(2)}, u32[]{:S(2)}) collective-permute-start(f32[1,1,1024]{2,1,0:T(1,128)S(1)} %slice_bitcast_fusion.8), channel_id=1, source_target_pairs={{0,256},{1,257},{2,258},{3,259},{4,260},{5,261},{6,262},{7,263},{8... | collective-permute-start | bytes 12296 | tf_op jit(solution)/shard_map/ppermute | solution.py:16
  83.2 15.8 %collective-permute-start.8 = (f32[1,64,32]{2,1,0:T(8,128)S(1)}, f32[1,64,32]{2,1,0:T(8,128)S(1)}, u32[]{:S(2)}, u32[]{:S(2)}) collective-permute-start(f32[1,64,32]{2,1,0:T(8,128)S(1)} %slice_bitcast_fusion.3), channel_id=1, source_target_pairs={{128,0},{129,1},{130,2},{131,3},{132,4},{133,5},{134,6},{135,7},{1... | collective-permute-start | bytes 24584 | tf_op jit(solution)/shard_map/ppermute | solution.py:16
  87.6 14.6 %collective-permute-start.14 = (f32[1,64,32]{2,1,0:T(8,128)S(1)}, f32[1,64,32]{2,1,0:T(8,128)S(1)}, u32[]{:S(2)}, u32[]{:S(2)}) collective-permute-start(f32[1,64,32]{2,1,0:T(8,128)S(1)} %copy-done.34), channel_id=1, source_target_pairs={{0,128},{1,129},{2,130},{3,131},{4,132},{5,133},{6,134},{7,135},{8... | collective-permute-start | bytes 24584 | tf_op jit(solution)/shard_map/ppermute | solution.py:16
  88.9 13.2 %collective-permute-start.15 = (f32[1,64,32]{2,1,0:T(8,128)S(1)}, f32[1,64,32]{2,1,0:T(8,128)S(1)}, u32[]{:S(2)}, u32[]{:S(2)}) collective-permute-start(f32[1,64,32]{2,1,0:T(8,128)S(1)} %slice_bitcast_fusion), channel_id=1, source_target_pairs={{128,0},{129,1},{130,2},{131,3},{132,4},{133,5},{134,6},{135,7},{1... | collective-permute-start | bytes 24584 | tf_op jit(solution)/shard_map/ppermute | solution.py:16
  92.9 9.2 %collective-permute-start.13 = (f32[1,1,1024]{2,1,0:T(1,128)S(1)}, f32[1,1,1024]{2,1,0:T(1,128)S(1)}, u32[]{:S(2)}, u32[]{:S(2)}) collective-permute-start(f32[1,1,1024]{2,1,0:T(1,128)S(1)} %copy-done.41), channel_id=1, source_target_pairs={{256,0},{257,1},{258,2},{259,3},{260,4},{261,5},{262,6},{263,7},{2... | collective-permute-start | bytes 12296 | tf_op jit(solution)/shard_map/ppermute | solution.py:16
  96.8 10.4 %collective-permute-start.17 = (f32[1,64,32]{1,2,0:T(8,128)S(1)}, f32[1,64,32]{1,2,0:T(8,128)S(1)}, u32[]{:S(2)}, u32[]{:S(2)}) collective-permute-start(f32[1,64,32]{1,2,0:T(8,128)S(1)} %fusion.45), channel_id=1, source_target_pairs={{1,0},{2,1},{3,2},{4,3},{5,4},{6,5},{7,6},{8,7},{9,8},{10,9},{11,1... | collective-permute-start | bytes 24584 | tf_op jit(solution)/shard_map/ppermute | solution.py:16
  99.0 3.2 %collective-permute-start.12 = (f32[1,1,1024]{2,1,0:T(1,128)S(1)}, f32[1,1,1024]{2,1,0:T(1,128)S(1)}, u32[]{:S(2)}, u32[]{:S(2)}) collective-permute-start(f32[1,1,1024]{2,1,0:T(1,128)S(1)} %copy-done.40), channel_id=1, source_target_pairs={{0,256},{1,257},{2,258},{3,259},{4,260},{5,261},{6,262},{7,263},{8... | collective-permute-start | bytes 12296 | tf_op jit(solution)/shard_map/ppermute | solution.py:16
  (44 other events, 444.4 us)
where the time goes:
time: 122 us; the launch traced here: 121 us
  starting transfers between devices  58 us (48%)
  local copies, waits for them, and re-layouts  32.4 us (27%)
  matrix products  15.3 us (13%)
  other arithmetic  8.81 us (7%)
  waiting for transfers between devices  5.07 us (4%)
  between operations  1.71 us (1%)
    ppermute x18, starting transfers between devices, passed_along(): return lax.ppermute(array, axis, pairs)  58 us
    squeeze x9, local copies, waits for them, and re-layouts, on_device(): final_local = [final_block[number] for number in range(7)]  9.05 us
    dot_general x3, matrix products, place_face(): jnp.dot(face, selector(EDGE - 1).T, precision=lax.Precision.HIGHEST, pref...  5.55 us
    ppermute x18, waiting for transfers between devices, passed_along(): return lax.ppermute(array, axis, pairs)  5.07 us
    dot_general x6, matrix products, take_face(): jnp.dot(field, picker, precision=lax.Precision.HIGHEST, preferred_element...  4.93 us
    dot_general x3, matrix products, place_face(): jnp.dot(face, selector(0).T, precision=lax.Precision.HIGHEST, preferred_e...  4.87 us
    unnamed x106, local copies, waits for them, and re-layouts  4.59 us
    squeeze x7, local copies, waits for them, and re-layouts, on_device(): state_first = [first_block[number] for number in range(7)]  2.98 us
  transfers between devices with their start and end apart: 18, of which 1 were waited for; matrix products, arithmetic and copies ran while one was open for 33% of the time, Pallas kernels for 0%

commit v1 on v0

v1 whole, which is shorter than its diff:
```python
import functools

import jax
import jax.numpy as jnp
from jax import lax
from jax.experimental import pallas as pl
from jax.experimental.pallas import tpu as pltpu
from jax.sharding import PartitionSpec as P

EDGE = 32
FLUID_KAPPA = 1.0 / 6.0
MESH = pl.DeviceIdType.MESH
F32 = jnp.float32
LAYERS = 2 * EDGE
ROWS = 8 * LAYERS
PARTS = (6, 11, 10, 10, 2, 2, 2, 3, 3)


def masks():
    lane = lax.broadcasted_iota(jnp.int32, (8, 128), 1)
    sub = lax.broadcasted_iota(jnp.int32, (8, 128), 0)
    return lane & 31, lane >> 5, sub


def pick(flag, yes, no):
    return jnp.where(jnp.broadcast_to(flag, (8, 128)), yes, no)


def z_up(v, halo, kz):
    return jnp.where(kz == 31, halo, pltpu.roll(v, 127, 1))


def z_down(v, halo, kz):
    return jnp.where(kz == 0, halo, pltpu.roll(v, 1, 1))


def y_up(v, halo, grp, sub):
    r = pltpu.roll(v, 96, 1)
    inner = jnp.where(grp == 3, pltpu.roll(r, 7, 0), r)
    return jnp.where((grp == 3) & (sub == 7), halo, inner)


def y_down(v, halo, grp, sub):
    r = pltpu.roll(v, 32, 1)
    inner = jnp.where(grp == 0, pltpu.roll(r, 1, 0), r)
    return jnp.where((grp == 0) & (sub == 0), halo, inner)


def weighted(q, d):
    even = (q[1] + q[2]) + (q[3] + q[4]) + (q[5] + q[6])
    odd = d[0] * (q[1] - q[2]) + d[1] * (q[3] - q[4]) + d[2] * (q[5] - q[6])
    return 0.25 * q[0] + 0.125 * even + 0.5 * odd


def tile8(row):
    return pl.ds(pl.multiple_of(row, 8), 8)


def exchange(
    nz, pop_h, fin_h, vel_h, kap_h, sol_h, act_h,
    tf, tg, po, co, yh, zh, xh,
    popb, finb, velb, kapb, solb, actb, tv, zm, ym, zp,
    s0, s1, s2, s3, s4, s5, s6, s7, s8, r0, r1, r2, r3, r4, r5, r6, r7, r8,
    load_sem, send_sem, recv_sem,
):
    sends = (s0, s1, s2, s3, s4, s5, s6, s7, s8)
    gets = (r0, r1, r2, r3, r4, r5, r6, r7, r8)
    gx, gy, gz = lax.axis_index("gx"), lax.axis_index("gy"), lax.axis_index("gz")
    ox, oy, up, down = 1 - gx, 1 - gy, gz + 1, gz - 1
    peers = (
        (ox, gy, gz), (gx, oy, gz), (gx, gy, up), (gx, gy, down), (ox, oy, gz),
        (ox, gy, up), (ox, gy, down), (gx, oy, up), (gx, oy, down),
    )
    has_up, has_down = gz < nz - 1, gz > 0
    exists = (None, None, has_up, has_down, None, has_up, has_down, has_up, has_down)

    def guarded(k, act):
        if exists[k] is None:
            act()
        else:
            pl.when(exists[k])(act)

    barrier = pltpu.get_barrier_semaphore()
    for k in range(9):
        guarded(k, lambda k=k: pl.semaphore_signal(barrier, inc=1, device_id=peers[k], device_id_type=MESH))
    loads = [
        pltpu.make_async_copy(src, dst, load_sem.at[n])
        for n, (src, dst) in enumerate(
            ((act_h, actb), (fin_h, finb), (vel_h, velb), (kap_h, kapb), (sol_h, solb), (pop_h, popb))
        )
    ]
    for copy in loads:
        copy.start()

    kz, grp, sub = masks()
    zero = jnp.zeros((8, 128), F32)
    s_e, g_e = 7 * oy, 3 * oy
    s_c = lax.rem(s_e + 4, 8)
    i_e, p_e = 31 * ox, ox
    sgx, sgy = (1 - 2 * gx).astype(F32), (1 - 2 * gy).astype(F32)
    first_x, first_y = gx == 0, gy == 0
    fx, fy, bx, by = 1 + ox, 3 + oy, 1 + gx, 3 + gy
    zsign = jnp.where(kz == 0, -0.5, 0.5)

    @pl.when(gz == nz - 1)
    def _():
        for k in (2, 5, 7):
            gets[k][...] = jnp.zeros_like(gets[k])

    @pl.when(gz == 0)
    def _():
        for k in (3, 6, 8):
            gets[k][...] = jnp.zeros_like(gets[k])

    loads[1].wait()
    for n in range(7):
        tf[n, 16 : 16 + ROWS, :] = finb[n].astype(F32)
    for n in (1, 2):
        tf[n, pl.ds(0, 8, stride=2), :] = zero
        tf[n, pl.ds(1, 8, stride=2), :] = tf[n, pl.ds(16 * 32, 8, stride=2), :]
        tf[n, pl.ds(16 * 33, 8, stride=2), :] = tf[n, pl.ds(16 + 1, 8, stride=2), :]
        tf[n, pl.ds(16 * 33 + 1, 8, stride=2), :] = zero
        po[n, 0:8, :] = zero
        po[n, ROWS + 8 : ROWS + 16, :] = zero
    loads[2].wait()
    for n in range(3):
        tv[n] = velb[n].astype(F32)
    loads[5].wait()
    for n in range(7):
        tg[n] = popb[n].astype(F32)
    loads[0].wait()
    loads[3].wait()
    loads[4].wait()
    active = (actb[0, 0].astype(F32), actb[0, 1].astype(F32))

    def cell(i, p, a):
        near = [tf[n, pl.ds(16 * (i + 1) + p, 8, stride=2), :] for n in (0, 3, 4, 5, 6)]
        q = [
            near[0],
            tf[1, pl.ds(16 * (i + 2) + p, 8, stride=2), :],
            tf[2, pl.ds(16 * i + p, 8, stride=2), :],
            y_up(near[1], zero, grp, sub),
            y_down(near[2], zero, grp, sub),
            z_up(near[3], zero, kz),
            z_down(near[4], zero, kz),
        ]
        here = tile8(256 * p + 8 * i)
        solid = solb[here, :] > 0
        kappa = jnp.where(solid, kapb[here, :], FLUID_KAPPA)
        rate = 1.0 / (4.0 * kappa + 0.5)
        ar = a * rate
        b = a - ar
        d = [jnp.where(solid, 0.0, tv[n, pl.ds(16 * i + p, 8, stride=2), :]) for n in range(3)]
        return near, q, solid, rate, ar, b, d, ar * weighted(q, d)

    def layer(i, p):
        x = 32 * p + i
        near, q, solid, rate, ar, b, d, ars = cell(i, p, active[p])
        here = tile8(8 * x)
        padded = tile8(8 * x + 8)
        for n, c in enumerate((ar, b, d[0], d[1], d[2])):
            co[n, here, :] = c
        co[5, here, :] = jnp.where(solid, -4.0 * active[p] * rate * rate, 0.0)
        g = [tg[n, pl.ds(16 * i + p, 8, stride=2), :] for n in range(7)]
        total = ((g[0] + g[1]) + (g[2] + g[3])) + ((g[4] + g[5]) + g[6])
        w = ar * total
        post = [b * g[0] + 0.25 * w]
        for n in range(3):
            even, odd = 0.125 * w, 0.5 * (w * d[n])
            post.append(b * g[2 * n + 1] + (even + odd))
            post.append(b * g[2 * n + 2] + (even - odd))
        for n in range(7):
            po[n, padded, :] = post[n]
        to_y = ar * (0.125 + 0.5 * sgy * d[1])
        bottom = kz == 0
        zm[0, here, :] = jnp.where(bottom, near[3], near[4])
        zm[1, here, :] = jnp.where(bottom, post[6], post[5])
        zm[2, here, :] = ars + b * jnp.where(bottom, q[5], q[6])
        zm[3, here, :] = ar * (0.125 + zsign * d[2])
        zm[4, here, :] = jnp.where(sub == s_e, pick(first_y, near[2], near[1]), pltpu.roll(to_y, 4, 0))
        ym[0, here, :] = ars + b * pick(first_y, q[4], q[3])
        ym[1, here, :] = to_y

    def sweep(i, carry):
        layer(i, 0)
        layer(i, 1)
        return carry

    lax.fori_loop(0, 32, sweep, 0)

    a_e = jnp.where(first_x, active[1], active[0])
    near, q, solid, rate, ar, b, d, ars = cell(i_e, p_e, a_e)
    x_e = 63 * ox
    here_e = tile8(8 * x_e)
    to_x = ar * (0.125 + 0.5 * sgx * d[0])
    own_x = tf[fx, pl.ds(16 * (i_e + 1) + p_e, 8, stride=2), :]
    own_y = pick(first_y, near[2], near[1])
    s0[0] = own_x
    s0[1] = po[bx, tile8(8 * x_e + 8), :]
    s0[2] = ars + b * pick(first_x, q[2], q[1])
    s0[3] = to_x
    s0[4] = ym[1, here_e, :]
    s0[5] = zm[3, here_e, :]

    def pack_y(read):
        out = []
        for h in range(2):
            v = zero
            for g in range(4):
                rows = read(32 * h + 8 * g, h, 8 * g)
                v = jnp.where(grp == g, pltpu.roll(rows, lax.rem(32 * (g - g_e) + 128, 128), 1), v)
            out.append(v)
        return out

    def every8(ref, n, pad):
        return lambda x, h, i: ref[n, pl.ds(8 * (x + pad) + s_e, 8, stride=8), :]

    packs = (
        pack_y(lambda x, h, i: tf[fy, pl.ds(16 * (i + 1) + h + 2 * s_e, 8, stride=16), :]),
        pack_y(every8(po, by, 1)),
        pack_y(every8(ym, 0, 0)),
        pack_y(every8(ym, 1, 0)),
        pack_y(every8(zm, 3, 0)),
    )
    for n, pair in enumerate(packs):
        s1[2 * n] = pair[0]
        s1[2 * n + 1] = pair[1]

    def moved(v, lanes, rows):
        v = pltpu.roll(v, lax.rem(lanes + 256, 128), 1)
        return pltpu.roll(v, lax.rem(rows + 16, 8), 0)

    s1[10] = moved(to_x, 32 * (3 * ox - g_e), 7 * ox - s_e)

    for n in range(5):

        def gather(i, carry):
            out = []
            for p in range(2):
                v = pltpu.roll(zm[n, tile8(256 * p + 8 * i), :], i, 1)
                out.append(jnp.where(kz == i, v, carry[2 * p]))
                out.append(jnp.where(kz == ((i + 31) & 31), v, carry[2 * p + 1]))
            return tuple(out)

        b0, t0, b1, t1 = lax.fori_loop(0, 32, gather, (zero,) * 4)
        t0, t1 = pltpu.roll(t0, 97, 1), pltpu.roll(t1, 97, 1)
        if n < 4:
            s3[2 * n], s3[2 * n + 1], s2[2 * n], s2[2 * n + 1] = b0, b1, t0, t1
        else:
            second = (sub == lax.rem(s_e + 1, 8)) | (sub == lax.rem(s_c + 1, 8))
            for msg, line, lo, hi in ((s3, s8, b0, b1), (s2, s7, t0, t1)):
                both = jnp.where(second, pltpu.roll(hi, 1, 0), lo)
                msg[9] = both
                line[0] = both
    s3[8] = moved(to_x, i_e, 0)
    s2[8] = moved(to_x, i_e - 31, 0)

    s_o, g_o = 7 * gy, 3 * gy
    s4[0] = jnp.where((sub == s_o) & (grp == g_o), moved(own_y, 32 * (g_o - g_e), s_o - s_e), 0.0)
    s4[1] = jnp.where((sub == 7 * gx) & (grp == 3 * gx), moved(own_x, 32 * (3 * gx - g_e), 7 * gx - s_e), 0.0)
    z_e = zm[0, here_e, :]
    i_o = 31 * gx
    s6[0] = jnp.where(kz == 31, pltpu.roll(z_e, 31, 1), 0.0)
    s5[0] = jnp.where(kz == 0, pltpu.roll(z_e, 97, 1), 0.0)
    s6[1] = jnp.where(kz == i_o, moved(own_x, i_o, 0), 0.0)
    s5[1] = jnp.where(kz == i_o, moved(own_x, i_o - 31, 0), 0.0)
    zy = pack_y(every8(zm, 0, 0))
    for h in range(2):
        s8[1 + h] = jnp.where(kz == 31, pltpu.roll(zy[h], 31, 1), 0.0)
        s7[1 + h] = jnp.where(kz == 0, pltpu.roll(zy[h], 97, 1), 0.0)

    count = 3 + 3 * has_up.astype(jnp.int32) + 3 * has_down.astype(jnp.int32)
    pl.semaphore_wait(barrier, count)

    lands = (0, 1, 3, 2, 4, 6, 5, 8, 7)
    copies = [
        pltpu.make_async_remote_copy(
            src_ref=sends[k], dst_ref=gets[lands[k]], send_sem=send_sem.at[k], recv_sem=recv_sem.at[lands[k]],
            device_id=peers[k], device_id_type=MESH,
        )
        for k in range(9)
    ]
    for k in range(9):
        guarded(k, copies[k].start)

    def arrival(k):
        return pltpu.make_async_remote_copy(
            src_ref=sends[lands[k]], dst_ref=gets[k], send_sem=send_sem.at[k], recv_sem=recv_sem.at[k],
            device_id=peers[k], device_id_type=MESH,
        )

    for k in range(9):
        guarded(k, lambda k=k: arrival(k).wait_recv())

    hi_y, lo_y = oy.astype(F32), gy.astype(F32)
    hi_x, lo_x = ox.astype(F32), gx.astype(F32)
    mid_y = []
    for h in range(2):
        m = r1[4 + h] + r1[6 + h] * s1[h] + r1[8 + h] * (r7[1 + h] + r8[1 + h])
        mid_y.append(m + (hi_x if h == 1 else lo_x) * (r1[10] * r4[1]))
    for n, pair in enumerate(((r1[0], r1[1]), (r1[2], r1[3]), mid_y)):
        for h in range(2):
            for g in range(4):
                rows = pl.ds(32 * h + 8 * g, 8)
                yh[n, rows, :] = hi_y * pltpu.roll(pair[h], (32 * (3 - g)) % 128, 1)
                yh[3 + n, rows, :] = lo_y * pltpu.roll(pair[h], (32 * (0 - g)) % 128, 1)
    corner = (sub == s_e) & (grp == g_e)
    for base, msg, line, cross, own in ((0, r2, r7, r5, s2), (6, r3, r8, r6, s3)):
        for v in range(2):
            side = hi_x if v == 1 else lo_x
            m = msg[4 + v] + msg[6 + v] * own[v] + side * (msg[8] * cross[1])
            c = jnp.broadcast_to(msg[9, pl.ds(lax.rem(s_c + v, 8), 1), :], (8, 128))
            f = jnp.broadcast_to(line[0, pl.ds(lax.rem(s_o + v, 8), 1), :], (8, 128))
            f = pltpu.roll(f, lax.rem(32 * (g_e - g_o) + 128, 128), 1)
            zh[base + v] = msg[v]
            zh[base + 2 + v] = msg[2 + v]
            zh[base + 4 + v] = m + jnp.where(corner, c * f, 0.0)
    mid_x = r0[2] + r0[3] * s0[0] + r0[4] * r4[0] + r0[5] * (r5[0] + r6[0])
    xh[0] = hi_x * mid_x
    xh[1] = lo_x * mid_x
    tf[1, pl.ds(16 * 33 + 1, 8, stride=2), :] = hi_x * r0[0]
    tf[2, pl.ds(0, 8, stride=2), :] = lo_x * r0[0]
    po[2, ROWS + 8 : ROWS + 16, :] = hi_x * r0[1]
    po[1, 0:8, :] = lo_x * r0[1]
    for k in range(9):
        guarded(k, copies[k].wait_send)


CHUNKS = 4


def finish(tf, tg, po, co, yh, zh, xh, out_h, grad_h, mid, term, out, grad, out_sem, grad_sem):
    kz, grp, sub = masks()

    def row(n, x):
        return jnp.broadcast_to(yh[n, pl.ds(x, 1), :], (8, 128))

    def above(n, p, i):
        return pltpu.roll(zh[2 * n + p], 31 - i, 1)

    def below(n, p, i):
        return pltpu.roll(zh[6 + 2 * n + p], lax.rem(128 - i, 128), 1)

    mid[1, ROWS + 8 : ROWS + 16, :] = xh[0]
    mid[2, 0:8, :] = xh[1]

    def middle(i, p):
        x = 32 * p + i
        near = [tf[n, pl.ds(16 * (i + 1) + p, 8, stride=2), :] for n in (0, 3, 4, 5, 6)]
        q = [
            near[0],
            tf[1, pl.ds(16 * (i + 2) + p, 8, stride=2), :],
            tf[2, pl.ds(16 * i + p, 8, stride=2), :],
            y_up(near[1], row(0, x), grp, sub),
            y_down(near[2], row(3, x), grp, sub),
            z_up(near[3], above(0, p, i), kz),
            z_down(near[4], below(0, p, i), kz),
        ]
        here = tile8(8 * x)
        padded = tile8(8 * x + 8)
        ar, b = co[0, here, :], co[1, here, :]
        s = weighted(q, [co[n, here, :] for n in (2, 3, 4)])
        ars = ar * s
        for n in range(7):
            mid[n, padded, :] = ars + b * q[n]
        g = [
            po[0, padded, :],
            po[1, here, :],
            po[2, tile8(8 * x + 16), :],
            y_down(po[3, padded, :], row(4, x), grp, sub),
            y_up(po[4, padded, :], row(1, x), grp, sub),
            z_down(po[5, padded, :], below(1, p, i), kz),
            z_up(po[6, padded, :], above(1, p, i), kz),
        ]
        t = (s - q[0]) * g[0]
        for n in range(1, 7):
            t = t + (s - q[n]) * g[n]
        term[here, :] = t

    def sweep(i, carry):
        middle(i, 0)
        middle(i, 1)
        return carry

    lax.fori_loop(0, 32, sweep, 0)

    def first(i, p):
        x = 32 * p + i
        here = tile8(8 * x)
        padded = tile8(8 * x + 8)
        q = [
            mid[0, padded, :],
            mid[1, tile8(8 * x + 16), :],
            mid[2, here, :],
            y_up(mid[3, padded, :], row(2, x), grp, sub),
            y_down(mid[4, padded, :], row(5, x), grp, sub),
            z_up(mid[5, padded, :], above(2, p, i), kz),
            z_down(mid[6, padded, :], below(2, p, i), kz),
        ]
        ar, b = co[0, here, :], co[1, here, :]
        s = weighted(q, [co[n, here, :] for n in (2, 3, 4)])
        ars = ar * s
        at = tile8(8 * i)
        t = term[here, :]
        for n in range(7):
            out[n, p, at, :] = ars + b * q[n]
            t = t + (s - q[n]) * tg[n, pl.ds(16 * i + p, 8, stride=2), :]
        grad[p, at, :] = co[5, here, :] * t

    def last(i, carry):
        first(i, 0)
        first(i, 1)
        return carry

    copies = []
    step = 32 // CHUNKS
    for c in range(CHUNKS):
        lax.fori_loop(c * step, (c + 1) * step, last, 0)
        rows = pl.ds(8 * step * c, 8 * step)
        copies.append(pltpu.make_async_copy(out.at[:, :, rows, :], out_h.at[:, :, rows, :], out_sem.at[c]))
        copies.append(pltpu.make_async_copy(grad.at[:, rows, :], grad_h.at[:, rows, :], grad_sem.at[c]))
        copies[-2].start()
        copies[-1].start()
    for copy in copies:
        copy.wait()


def on_device(nz, populations, adjoint_final, velocity, particle_kappa, solid_label, tile_active):
    def paired(block):
        n = block.shape[0]
        return block.reshape(n, 2, 256, 128).transpose(0, 2, 1, 3).reshape(n, ROWS, 128)

    args = [
        paired(populations), paired(adjoint_final), paired(velocity),
        particle_kappa.reshape(ROWS, 128), solid_label.reshape(ROWS, 128), tile_active.reshape(1, 2),
    ]
    args = [pltpu.with_memory_space_constraint(a, pltpu.HBM) for a in args]
    hbm, vmem = pl.BlockSpec(memory_space=pltpu.HBM), pl.BlockSpec(memory_space=pltpu.VMEM)
    kept = [
        pltpu.VMEM(shape, F32)
        for shape in (
            (7, ROWS + 32, 128), (7, ROWS, 128), (7, ROWS + 16, 128), (6, ROWS, 128),
            (6, LAYERS, 128), (12, 8, 128), (2, 8, 128),
        )
    ]
    messages = [pltpu.VMEM((n, 8, 128), F32) for n in PARTS]
    held = pl.pallas_call(
        functools.partial(exchange, nz),
        out_shape=kept,
        in_specs=[hbm] * 6,
        out_specs=[vmem] * 7,
        scratch_shapes=[
            pltpu.VMEM((7, ROWS, 128), jnp.bfloat16),
            pltpu.VMEM((7, ROWS, 128), jnp.bfloat16),
            pltpu.VMEM((3, ROWS, 128), jnp.bfloat16),
            pltpu.VMEM((ROWS, 128), F32),
            pltpu.VMEM((ROWS, 128), jnp.int32),
            pltpu.SMEM((1, 2), jnp.int32),
            pltpu.VMEM((3, ROWS, 128), F32),
            pltpu.VMEM((5, ROWS, 128), F32),
            pltpu.VMEM((2, ROWS, 128), F32),
            pltpu.VMEM((4, 8, 128), F32),
            *messages,
            *messages,
            pltpu.SemaphoreType.DMA((6,)),
            pltpu.SemaphoreType.DMA((9,)),
            pltpu.SemaphoreType.DMA((9,)),
        ],
        compiler_params=pltpu.CompilerParams(
            collective_id=0, has_side_effects=True, vmem_limit_bytes=24 * 2**20
        ),
        name="exchange",
    )(*args)
    first, gradient = pl.pallas_call(
        finish,
        out_shape=[
            jax.ShapeDtypeStruct((7, 2, 256, 128), F32),
            jax.ShapeDtypeStruct((2, 256, 128), F32),
        ],
        in_specs=[vmem] * 7,
        out_specs=[hbm] * 2,
        scratch_shapes=[
            pltpu.VMEM((7, ROWS + 16, 128), F32),
            pltpu.VMEM((ROWS, 128), F32),
            pltpu.VMEM((7, 2, 256, 128), F32),
            pltpu.VMEM((2, 256, 128), F32),
            pltpu.SemaphoreType.DMA((CHUNKS,)),
            pltpu.SemaphoreType.DMA((CHUNKS,)),
        ],
        compiler_params=pltpu.CompilerParams(vmem_limit_bytes=24 * 2**20),
        name="finish",
    )(*held)
    voxels = EDGE * EDGE * EDGE
    return first.reshape(7, 2, 1, 1, voxels), gradient.reshape(2, 1, 1, voxels)


def solution(mesh):
    spec, one = P(None, "gx", "gy", "gz", None), P("gx", "gy", "gz", None)
    return jax.shard_map(
        functools.partial(on_device, mesh.shape["gz"]),
        mesh=mesh,
        in_specs=(spec, spec, spec, one, one, P("gx", "gy", "gz")),
        out_specs=(spec, one),
        check_vma=False,
    )
```

time: 122 us -> 34.4 us (0.28)
  the two profiles are of different devices: /device:TPU:255 before, /device:TPU:4 now
where the time goes in v1:
time: 34.4 us; the launch traced here: 34 us
  Pallas kernels  33.3 us (97%)
  between operations  0.64 us (2%)
    pallas_call x1, Pallas kernels, on_device(): pl.pallas_call(functools.partial(exchange, nz), out_shape=kept, in_specs=...  26.2 us
    pallas_call x1, Pallas kernels, on_device(): pl.pallas_call(finish, out_shape=[jax.ShapeDtypeStruct((7, 2, 256, 128),...  7.18 us

profile of v1, /device:TPU:4, one launch (start us, length us, event | category | flops | bytes accessed | tf_op | source)
XLA Modules:
  0.0 34.0 jit_solution(3415643404966572967)
XLA Ops:
  0.6 26.2 %exchange.1 = (f32[7,544,128]{2,1,0:T(8,128)S(1)}, f32[7,512,128]{2,1,0:T(8,128)S(1)}, f32[7,528,128]{2,1,0:T(8,128)S(1)}, f32[6,512,128]{2,1,0:T(8,128)S(1)}, f...) custom-call(bf16[7,512,128]{2,1,0:T(8,128)(2,1)} %bitcast.20, ...), custom_call_target="tpu_custom_call" | custom-call | tf_op jit(solution)/shard_map/exchange/pallas_call | solution.py:447
  26.8 7.2 %finish.1 = (f32[7,2,256,128]{3,2,1,0:T(8,128)}, f32[2,256,128]{2,1,0:T(8,128)}) custom-call(f32[7,544,128]{2,1,0:T(8,128)S(1)} %get-tuple-element.11.tf, f32[7,512,128]{2,1,0:T(8,128)S(1)} %get-tuple-element.12.tg, f32[7,528,128]{2,1,0:T(8,128)S(1)} %get-tuple-element.13.po, f32[6,512,128]{2,1,0:T(8,128)S(1)} %get-tuple-element.14.co, ...), custom_call_target="tpu_custom_call" | custom-call | tf_op jit(solution)/shard_map/finish/pallas_call | solution.py:474

commit v2 on v1

--- a/solution.py
+++ b/solution.py
@@ -186,7 +186,7 @@
         layer(i, 1)
         return carry
 
-    lax.fori_loop(0, 32, sweep, 0)
+    lax.fori_loop(0, 32, sweep, 0, unroll=8)
 
     a_e = jnp.where(first_x, active[1], active[0])
     near, q, solid, rate, ar, b, d, ars = cell(i_e, p_e, a_e)
@@ -234,15 +234,13 @@
 
     for n in range(5):
 
-        def gather(i, carry):
-            out = []
-            for p in range(2):
-                v = pltpu.roll(zm[n, tile8(256 * p + 8 * i), :], i, 1)
-                out.append(jnp.where(kz == i, v, carry[2 * p]))
-                out.append(jnp.where(kz == ((i + 31) & 31), v, carry[2 * p + 1]))
-            return tuple(out)
-
-        b0, t0, b1, t1 = lax.fori_loop(0, 32, gather, (zero,) * 4)
+        b0, t0, b1, t1 = (zero,) * 4
+        for i in range(32):
+            v0 = pltpu.roll(zm[n, 8 * i : 8 * i + 8, :], i, 1)
+            v1 = pltpu.roll(zm[n, 256 + 8 * i : 264 + 8 * i, :], i, 1)
+            bottom, top = kz == i, kz == (i + 31) % 32
+            b0, t0 = jnp.where(bottom, v0, b0), jnp.where(top, v0, t0)
+            b1, t1 = jnp.where(bottom, v1, b1), jnp.where(top, v1, t1)
         t0, t1 = pltpu.roll(t0, 97, 1), pltpu.roll(t1, 97, 1)
         if n < 4:
             s3[2 * n], s3[2 * n + 1], s2[2 * n], s2[2 * n + 1] = b0, b1, t0, t1
@@ -382,7 +380,7 @@
         middle(i, 1)
         return carry
 
-    lax.fori_loop(0, 32, sweep, 0)
+    lax.fori_loop(0, 32, sweep, 0, unroll=8)
 
     def first(i, p):
         x = 32 * p + i
@@ -415,7 +413,7 @@
     copies = []
     step = 32 // CHUNKS
     for c in range(CHUNKS):
-        lax.fori_loop(c * step, (c + 1) * step, last, 0)
+        lax.fori_loop(c * step, (c + 1) * step, last, 0, unroll=8)
         rows = pl.ds(8 * step * c, 8 * step)
         copies.append(pltpu.make_async_copy(out.at[:, :, rows, :], out_h.at[:, :, rows, :], out_sem.at[c]))
         copies.append(pltpu.make_async_copy(grad.at[:, rows, :], grad_h.at[:, rows, :], grad_sem.at[c]))

time: 34.4 us -> 17.6 us (0.51)
  the two profiles are of different devices: /device:TPU:4 before, /device:TPU:1 now
where the time goes in v2:
time: 17.6 us; the launch traced here: 17.5 us
  Pallas kernels  16.8 us (95%)
  between operations  0.64 us (4%)
    pallas_call x1, Pallas kernels, on_device(): pl.pallas_call(functools.partial(exchange, nz), out_shape=kept, in_specs=...  14.1 us
    pallas_call x1, Pallas kernels, on_device(): pl.pallas_call(finish, out_shape=[jax.ShapeDtypeStruct((7, 2, 256, 128),...  2.76 us

profile of v2, /device:TPU:1, one launch (start us, length us, event | category | flops | bytes accessed | tf_op | source)
XLA Modules:
  0.0 17.5 jit_solution(9322601990674694616)
XLA Ops:
  0.6 14.1 %exchange.1 = (f32[7,544,128]{2,1,0:T(8,128)S(1)}, f32[7,512,128]{2,1,0:T(8,128)S(1)}, f32[7,528,128]{2,1,0:T(8,128)S(1)}, f32[6,512,128]{2,1,0:T(8,128)S(1)}, f...) custom-call(bf16[7,512,128]{2,1,0:T(8,128)(2,1)} %bitcast.20, ...), custom_call_target="tpu_custom_call" | custom-call | tf_op jit(solution)/shard_map/exchange/pallas_call | solution.py:445
  14.7 2.8 %finish.1 = (f32[7,2,256,128]{3,2,1,0:T(8,128)}, f32[2,256,128]{2,1,0:T(8,128)}) custom-call(f32[7,544,128]{2,1,0:T(8,128)S(1)} %get-tuple-element.11.tf, f32[7,512,128]{2,1,0:T(8,128)S(1)} %get-tuple-element.12.tg, f32[7,528,128]{2,1,0:T(8,128)S(1)} %get-tuple-element.13.po, f32[6,512,128]{2,1,0:T(8,128)S(1)} %get-tuple-element.14.co, ...), custom_call_target="tpu_custom_call" | custom-call | tf_op jit(solution)/shard_map/finish/pallas_call | solution.py:472

commit v3 on v2

v3 whole, which is shorter than its diff:
```python
import functools

import jax
import jax.numpy as jnp
from jax import lax
from jax.experimental import pallas as pl
from jax.experimental.pallas import tpu as pltpu
from jax.sharding import PartitionSpec as P

EDGE = 32
FLUID_KAPPA = 1.0 / 6.0
MESH = pl.DeviceIdType.MESH
F32 = jnp.float32
LAYERS = 2 * EDGE
ROWS = 8 * LAYERS
PARTS = (48, 73, 74, 74, 2, 8, 8, 10, 10)


def masks():
    lane = lax.broadcasted_iota(jnp.int32, (8, 128), 1)
    sub = lax.broadcasted_iota(jnp.int32, (8, 128), 0)
    return lane & 31, lane >> 5, sub


def pick(flag, yes, no):
    return jnp.where(jnp.broadcast_to(flag, (8, 128)), yes, no)


def z_up(v, halo, kz):
    return jnp.where(kz == 31, halo, pltpu.roll(v, 127, 1))


def z_down(v, halo, kz):
    return jnp.where(kz == 0, halo, pltpu.roll(v, 1, 1))


def y_up(v, after, halo, grp, sub):
    return pltpu.roll(jnp.where(grp == 0, jnp.where(sub == 7, halo, after), v), 96, 1)


def y_down(v, before, halo, grp, sub):
    return pltpu.roll(jnp.where(grp == 3, jnp.where(sub == 0, halo, before), v), 32, 1)


def weighted(q, d):
    even = (q[1] + q[2]) + (q[3] + q[4]) + (q[5] + q[6])
    odd = d[0] * (q[1] - q[2]) + d[1] * (q[3] - q[4]) + d[2] * (q[5] - q[6])
    return 0.25 * q[0] + 0.125 * even + 0.5 * odd


def part(n):
    return slice(8 * n, 8 * n + 8)


def tile8(row):
    return pl.ds(pl.multiple_of(row, 8), 8)


def exchange(
    nz, pop_h, fin_h, vel_h, kap_h, sol_h, act_h,
    tf, tg, po, co, yh, zh, xh,
    popb, finb, velb, kapb, solb, actb, tv, zm, ym, zp,
    s0, s1, s2, s3, s4, s5, s6, s7, s8, r0, r1, r2, r3, r4, r5, r6, r7, r8,
    load_sem, send_sem, recv_sem, ready,
):
    sends = (s0, s1, s2, s3, s4, s5, s6, s7, s8)
    gets = (r0, r1, r2, r3, r4, r5, r6, r7, r8)
    gx, gy, gz = lax.axis_index("gx"), lax.axis_index("gy"), lax.axis_index("gz")
    ox, oy, up, down = 1 - gx, 1 - gy, gz + 1, gz - 1
    peers = (
        (ox, gy, gz), (gx, oy, gz), (gx, gy, up), (gx, gy, down), (ox, oy, gz),
        (ox, gy, up), (ox, gy, down), (gx, oy, up), (gx, oy, down),
    )
    has_up, has_down = gz < nz - 1, gz > 0
    exists = (None, None, has_up, has_down, None, has_up, has_down, has_up, has_down)
    root = (gx == 0) & (gy == 0) & (gz == 0)
    other = jnp.logical_not(root)
    to_root = [(x == 0) & (y == 0) & (z == 0) for x, y, z in peers]

    def guarded(k, act, also=None):
        flag = exists[k]
        if also is not None:
            flag = also if flag is None else flag & also
        if flag is None:
            act()
        else:
            pl.when(flag)(act)

    barrier = pltpu.get_barrier_semaphore()

    def signal(k, semaphore):
        return lambda: pl.semaphore_signal(semaphore, inc=1, device_id=peers[k], device_id_type=MESH)

    for k in range(9):
        guarded(k, signal(k, barrier), other)
    count = 3 + 3 * has_up.astype(jnp.int32) + 3 * has_down.astype(jnp.int32)
    near_root = functools.reduce(jnp.logical_or, to_root)
    loads = [
        pltpu.make_async_copy(src, dst, load_sem.at[n])
        for n, (src, dst) in enumerate(
            ((act_h, actb), (fin_h, finb), (vel_h, velb), (kap_h, kapb), (sol_h, solb), (pop_h, popb))
        )
    ]
    for copy in loads:
        copy.start()

    @pl.when(root)
    def _():
        pl.semaphore_wait(barrier, count)
        for k in range(9):
            guarded(k, signal(k, ready))

    lands = (0, 1, 3, 2, 4, 6, 5, 8, 7)
    copies = [
        pltpu.make_async_remote_copy(
            src_ref=sends[k], dst_ref=gets[lands[k]], send_sem=send_sem.at[k], recv_sem=recv_sem.at[lands[k]],
            device_id=peers[k], device_id_type=MESH,
        )
        for k in range(9)
    ]

    kz, grp, sub = masks()
    zero = jnp.zeros((8, 128), F32)
    s_e, g_e = 7 * oy, 3 * oy
    s_c = lax.rem(s_e + 4, 8)
    i_e, p_e = 31 * ox, ox
    sgx, sgy = (1 - 2 * gx).astype(F32), (1 - 2 * gy).astype(F32)
    first_x, first_y = gx == 0, gy == 0
    fx, fy, bx, by = 1 + ox, 3 + oy, 1 + gx, 3 + gy
    zsign = jnp.where(kz == 0, -0.5, 0.5)

    @pl.when(gz == nz - 1)
    def _():
        for k in (2, 5, 7):
            gets[k][...] = jnp.zeros_like(gets[k])

    @pl.when(gz == 0)
    def _():
        for k in (3, 6, 8):
            gets[k][...] = jnp.zeros_like(gets[k])

    loads[1].wait()
    for n in range(7):
        tf[n, 16 : 16 + ROWS, :] = finb[n].astype(F32)
    for n in (1, 2):
        tf[n, pl.ds(0, 8, stride=2), :] = zero
        tf[n, pl.ds(1, 8, stride=2), :] = tf[n, pl.ds(16 * 32, 8, stride=2), :]
        tf[n, pl.ds(16 * 33, 8, stride=2), :] = tf[n, pl.ds(16 + 1, 8, stride=2), :]
        tf[n, pl.ds(16 * 33 + 1, 8, stride=2), :] = zero
        po[n, 0:8, :] = zero
        po[n, ROWS + 8 : ROWS + 16, :] = zero
    loads[2].wait()
    for n in range(3):
        tv[n] = velb[n].astype(F32)
    loads[5].wait()
    for n in range(7):
        tg[n] = popb[n].astype(F32)
    loads[0].wait()
    loads[3].wait()
    loads[4].wait()
    active = (actb[0, 0].astype(F32), actb[0, 1].astype(F32))

    def cell(i, p, a):
        near = [tf[n, pl.ds(16 * (i + 1) + p, 8, stride=2), :] for n in (0, 3, 4, 5, 6)]
        q = [
            near[0],
            tf[1, pl.ds(16 * (i + 2) + p, 8, stride=2), :],
            tf[2, pl.ds(16 * i + p, 8, stride=2), :],
            y_up(near[1], tf[3, pl.ds(16 * (i + 1) + p + 2, 8, stride=2), :], zero, grp, sub),
            y_down(near[2], tf[4, pl.ds(16 * (i + 1) + p - 2, 8, stride=2), :], zero, grp, sub),
            z_up(near[3], zero, kz),
            z_down(near[4], zero, kz),
        ]
        here = tile8(256 * p + 8 * i)
        solid = solb[here, :] > 0
        kappa = jnp.where(solid, kapb[here, :], FLUID_KAPPA)
        rate = 1.0 / (4.0 * kappa + 0.5)
        ar = a * rate
        b = a - ar
        d = [jnp.where(solid, 0.0, tv[n, pl.ds(16 * i + p, 8, stride=2), :]) for n in range(3)]
        return near, q, solid, rate, ar, b, d, ar * weighted(q, d)

    def layer(i, p, a):
        x = 32 * p + i
        near, q, solid, rate, ar, b, d, ars = cell(i, p, a)
        here = tile8(8 * x)
        padded = tile8(8 * x + 8)
        for n, c in enumerate((ar, b, d[0], d[1], d[2])):
            co[n, here, :] = c
        co[5, here, :] = jnp.where(solid, -4.0 * a * rate * rate, 0.0)
        g = [tg[n, pl.ds(16 * i + p, 8, stride=2), :] for n in range(7)]
        total = ((g[0] + g[1]) + (g[2] + g[3])) + ((g[4] + g[5]) + g[6])
        w = ar * total
        post = [b * g[0] + 0.25 * w]
        for n in range(3):
            even, odd = 0.125 * w, 0.5 * (w * d[n])
            post.append(b * g[2 * n + 1] + (even + odd))
            post.append(b * g[2 * n + 2] + (even - odd))
        for n in range(7):
            po[n, padded, :] = post[n]
        to_y = ar * (0.125 + 0.5 * sgy * d[1])
        bottom = kz == 0
        zm[0, here, :] = jnp.where(bottom, near[3], near[4])
        zm[1, here, :] = jnp.where(bottom, post[6], post[5])
        zm[2, here, :] = ars + b * jnp.where(bottom, q[5], q[6])
        zm[3, here, :] = ar * (0.125 + zsign * d[2])
        zm[4, here, :] = jnp.where(sub == s_e, pick(first_y, near[2], near[1]), pltpu.roll(to_y, 4, 0))
        ym[0, here, :] = ars + b * pick(first_y, q[4], q[3])
        ym[1, here, :] = to_y
        return near, q, ar, b, d, ars

    def sweep(i, carry):
        layer(i, 0, active[0])
        layer(i, 1, active[1])
        return carry

    a_e = jnp.where(first_x, active[1], active[0])
    near, q, ar, b, d, ars = layer(i_e, p_e, a_e)
    x_e = 63 * ox
    here_e = tile8(8 * x_e)
    to_x = ar * (0.125 + 0.5 * sgx * d[0])
    own_x = tf[fx, pl.ds(16 * (i_e + 1) + p_e, 8, stride=2), :]
    own_y = pick(first_y, near[2], near[1])
    s0[part(0)] = own_x
    s0[part(1)] = po[bx, tile8(8 * x_e + 8), :]
    s0[part(2)] = ars + b * pick(first_x, q[2], q[1])
    s0[part(3)] = to_x
    s0[part(4)] = ym[1, here_e, :]
    s0[part(5)] = zm[3, here_e, :]
    pl.when(root)(copies[0].start)

    lax.fori_loop(0, 32, sweep, 0, unroll=8)

    def pack_y(read):
        out = []
        for h in range(2):
            v = zero
            for g in range(4):
                rows = read(32 * h + 8 * g, h, 8 * g)
                v = jnp.where(grp == g, pltpu.roll(rows, lax.rem(32 * (g - g_e) + 128, 128), 1), v)
            out.append(v)
        return out

    def every8(ref, n, pad):
        return lambda x, h, i: ref[n, pl.ds(8 * (x + pad) + s_e, 8, stride=8), :]

    packs = (
        pack_y(lambda x, h, i: tf[fy, pl.ds(16 * (i + 1) + h + 2 * s_e, 8, stride=16), :]),
        pack_y(every8(po, by, 1)),
        pack_y(every8(ym, 0, 0)),
        pack_y(every8(ym, 1, 0)),
        pack_y(every8(zm, 3, 0)),
    )
    for n, pair in enumerate(packs[:4]):
        s1[part(2 * n)] = pair[0]
        s1[part(2 * n + 1)] = pair[1]
    s1[part(8)] = jnp.where((kz == 7) | (kz == 8), pltpu.roll(packs[4][1], 8, 1), packs[4][0])

    def shifted(v, lanes):
        return pltpu.roll(v, lax.rem(lanes + 256, 128), 1)

    zp[0] = shifted(to_x, 32 * (3 * ox - g_e))
    s1[72:73, :] = zp[0, pl.ds(s_e, 1), :]

    for n in range(5):

        b0, t0, b1, t1 = (zero,) * 4
        for i in range(32):
            v0 = pltpu.roll(zm[n, 8 * i : 8 * i + 8, :], i, 1)
            v1 = pltpu.roll(zm[n, 256 + 8 * i : 264 + 8 * i, :], i, 1)
            bottom, top = kz == i, kz == (i + 31) % 32
            b0, t0 = jnp.where(bottom, v0, b0), jnp.where(top, v0, t0)
            b1, t1 = jnp.where(bottom, v1, b1), jnp.where(top, v1, t1)
        t0, t1 = pltpu.roll(t0, 97, 1), pltpu.roll(t1, 97, 1)
        if n < 4:
            for msg, v, value in ((s3, 0, b0), (s3, 1, b1), (s2, 0, t0), (s2, 1, t1)):
                msg[part(2 * n + v)] = value
        else:
            for v, line in enumerate((b0, b1, t0, t1)):
                zp[1 + v] = line
            for v, (msg, other_msg) in enumerate(((s3, s8), (s2, s7))):
                for h in range(2):
                    msg[72 + h : 73 + h, :] = zp[1 + 2 * v + h, pl.ds(s_c, 1), :]
                    other_msg[8 + h : 9 + h, :] = zp[1 + 2 * v + h, pl.ds(s_e, 1), :]
    s3[part(8)] = shifted(to_x, i_e)
    s2[part(8)] = shifted(to_x, i_e - 31)

    s_o, g_o = 7 * gy, 3 * gy
    zp[5] = jnp.where(grp == g_o, shifted(own_y, 32 * (g_o - g_e)), 0.0)
    zp[6] = jnp.where(grp == 3 * gx, shifted(own_x, 32 * (3 * gx - g_e)), 0.0)
    s4[0:1, :] = zp[5, pl.ds(s_e, 1), :]
    s4[1:2, :] = zp[6, pl.ds(s_e, 1), :]
    z_e = zm[0, here_e, :]
    s6[...] = jnp.where(kz == 16, pltpu.roll(own_x, 16, 1), pltpu.roll(z_e, 31, 1))
    s5[...] = jnp.where(kz == 16, pltpu.roll(own_x, 113, 1), pltpu.roll(z_e, 97, 1))
    zy = pack_y(every8(zm, 0, 0))
    s8[0:8, :] = jnp.where(kz == 7, pltpu.roll(zy[1], 39, 1), pltpu.roll(zy[0], 31, 1))
    s7[0:8, :] = jnp.where(kz == 8, pltpu.roll(zy[1], 105, 1), pltpu.roll(zy[0], 97, 1))

    order = (4, 5, 6, 7, 8, 1, 2, 3, 0)

    @pl.when(root)
    def _():
        for k in order[:-1]:
            guarded(k, copies[k].start)

    @pl.when(other)
    def _():
        pl.semaphore_wait(barrier, count - near_root.astype(jnp.int32))
        for k in order:
            guarded(k, copies[k].start, jnp.logical_not(to_root[k]))

    @pl.when(near_root)
    def _():
        pl.semaphore_wait(ready, 1)
        for k in order:
            pl.when(to_root[k])(copies[k].start)

    def arrival(k):
        return pltpu.make_async_remote_copy(
            src_ref=sends[lands[k]], dst_ref=gets[k], send_sem=send_sem.at[k], recv_sem=recv_sem.at[k],
            device_id=peers[k], device_id_type=MESH,
        )

    for k in range(9):
        guarded(k, lambda k=k: arrival(k).wait_recv())

    hi_x, lo_x = ox.astype(F32), gx.astype(F32)

    def spread(row):
        return jnp.broadcast_to(row, (8, 128))

    top, bottom = kz == 31, kz == 0
    line_y = jnp.where(sub == 7 * ox, spread(r4[1:2, :]), 0.0)
    mid_y = []
    for h in range(2):
        edge = [r1[part(8)], r7[0:8, :], r8[0:8, :]]
        if h == 1:
            edge = [pltpu.roll(v, 120, 1) for v in edge]
        m = r1[part(4 + h)] + r1[part(6 + h)] * s1[part(h)]
        m = m + edge[0] * (jnp.where(top, edge[1], 0.0) + jnp.where(bottom, edge[2], 0.0))
        mid_y.append(m + (hi_x if h == 1 else lo_x) * (spread(r1[72:73, :]) * line_y))
    for n, pair in enumerate(((r1[part(0)], r1[part(1)]), (r1[part(2)], r1[part(3)]), mid_y)):
        for h in range(2):
            for g in range(4):
                yh[n, pl.ds(32 * h + 8 * g, 8), :] = pltpu.roll(pair[h], lax.rem(32 * (g_o - g) + 128, 128), 1)
    corner = (sub == s_e) & (grp == g_e)
    for base, msg, line, cross, own in ((0, r2, r7, r5, s2), (6, r3, r8, r6, s3)):
        line_z = jnp.where(kz == i_e, shifted(cross[...], i_e - 16), 0.0)
        for v in range(2):
            side = hi_x if v == 1 else lo_x
            m = msg[part(4 + v)] + msg[part(6 + v)] * own[part(v)] + side * (msg[part(8)] * line_z)
            f = shifted(spread(line[8 + v : 9 + v, :]), 32 * (g_e - g_o))
            m = m + jnp.where(corner, spread(msg[72 + v : 73 + v, :]) * f, 0.0)
            for n, halo in enumerate((msg[part(v)], msg[part(2 + v)], m)):
                zh[base + 2 * n + v] = halo if base == 0 else pltpu.roll(halo, 97, 1)
    mid_x = r0[part(2)] + r0[part(3)] * s0[part(0)]
    mid_x = mid_x + r0[part(4)] * jnp.where(sub == s_e, spread(r4[0:1, :]), 0.0)
    mid_x = mid_x + r0[part(5)] * (jnp.where(top, r5[...], 0.0) + jnp.where(bottom, r6[...], 0.0))
    xh[0] = hi_x * mid_x
    xh[1] = lo_x * mid_x
    tf[1, pl.ds(16 * 33 + 1, 8, stride=2), :] = hi_x * r0[part(0)]
    tf[2, pl.ds(0, 8, stride=2), :] = lo_x * r0[part(0)]
    po[2, ROWS + 8 : ROWS + 16, :] = hi_x * r0[part(1)]
    po[1, 0:8, :] = lo_x * r0[part(1)]
    for k in range(9):
        guarded(k, copies[k].wait_send)


BLOCK = 16
CHUNKS = LAYERS // BLOCK


def finish(tf, tg, po, co, yh, zh, xh, out_h, grad_h, mid, term, out, grad, out_sem, grad_sem):
    kz, grp, sub = masks()
    gy = lax.axis_index("gy")
    hi_y, lo_y = (1 - gy).astype(F32), gy.astype(F32)

    def row(n, x):
        r = jnp.broadcast_to(yh[n, x : x + 1, :], (8, 128))
        return hi_y * r, lo_y * r

    def both_z(n, p, i):
        return pltpu.roll(jnp.where(kz == i, zh[2 * n + p], zh[6 + 2 * n + p]), 31 - i, 1)

    mid[1, ROWS + 8 : ROWS + 16, :] = xh[0]
    mid[2, 0:8, :] = xh[1]

    def middle(x):
        p, i = x // 32, x % 32

        def near(n, rows):
            return tf[n, pl.ds(16 * (i + 1) + p + 2 * rows, 8, stride=2), :]

        hi, lo = row(0, x)
        hz = both_z(0, p, i)
        q = [
            near(0, 0),
            near(1, 8),
            near(2, -8),
            y_up(near(3, 0), near(3, 1), hi, grp, sub),
            y_down(near(4, 0), near(4, -1), lo, grp, sub),
            z_up(near(5, 0), hz, kz),
            z_down(near(6, 0), hz, kz),
        ]
        here = pl.ds(8 * x, 8)
        ar, b = co[0, here, :], co[1, here, :]
        s = weighted(q, [co[n, here, :] for n in (2, 3, 4)])
        ars = ar * s
        for n in range(7):
            mid[n, 8 * x + 8 : 8 * x + 16, :] = ars + b * q[n]

        def moved(n, rows):
            return po[n, pl.ds(8 * x + 8 + rows, 8), :]

        hi, lo = row(1, x)
        hz = both_z(1, p, i)
        g = [
            moved(0, 0),
            moved(1, -8),
            moved(2, 8),
            y_down(moved(3, 0), moved(3, -1), lo, grp, sub),
            y_up(moved(4, 0), moved(4, 1), hi, grp, sub),
            z_down(moved(5, 0), hz, kz),
            z_up(moved(6, 0), hz, kz),
        ]
        t = [(s - q[n]) * g[n] for n in range(7)]
        term[here, :] = ((t[0] + t[1]) + (t[2] + t[3])) + ((t[4] + t[5]) + t[6])

    def first(x):
        p, i = x // 32, x % 32

        def near(n, rows):
            return mid[n, pl.ds(8 * x + 8 + rows, 8), :]

        hi, lo = row(2, x)
        hz = both_z(2, p, i)
        q = [
            near(0, 0),
            near(1, 8),
            near(2, -8),
            y_up(near(3, 0), near(3, 1), hi, grp, sub),
            y_down(near(4, 0), near(4, -1), lo, grp, sub),
            z_up(near(5, 0), hz, kz),
            z_down(near(6, 0), hz, kz),
        ]
        here = pl.ds(8 * x, 8)
        ar, b = co[0, here, :], co[1, here, :]
        s = weighted(q, [co[n, here, :] for n in (2, 3, 4)])
        ars = ar * s
        at = pl.ds(8 * i, 8)
        for n in range(7):
            out[n, p, at, :] = ars + b * q[n]
        t = [(s - q[n]) * tg[n, pl.ds(16 * i + p, 8, stride=2), :] for n in range(7)]
        t = ((t[0] + t[1]) + (t[2] + t[3])) + ((t[4] + t[5]) + t[6])
        grad[p, at, :] = co[5, here, :] * (term[here, :] + t)

    middle(0)
    copies = []
    for c in range(CHUNKS):
        for x in range(BLOCK * c, BLOCK * (c + 1)):
            if x + 1 < LAYERS:
                middle(x + 1)
        for x in range(BLOCK * c, BLOCK * (c + 1)):
            first(x)
        p, i = BLOCK * c // 32, BLOCK * c % 32
        rows = pl.ds(8 * i, 8 * BLOCK)
        copies.append(pltpu.make_async_copy(out.at[:, p, rows, :], out_h.at[:, p, rows, :], out_sem.at[c]))
        copies.append(pltpu.make_async_copy(grad.at[p, rows, :], grad_h.at[p, rows, :], grad_sem.at[c]))
        copies[-2].start()
        copies[-1].start()
    for copy in copies:
        copy.wait()


def on_device(nz, populations, adjoint_final, velocity, particle_kappa, solid_label, tile_active):
    def paired(block):
        n = block.shape[0]
        return block.reshape(n, 2, 256, 128).transpose(0, 2, 1, 3).reshape(n, ROWS, 128)

    args = [
        paired(populations), paired(adjoint_final), paired(velocity),
        particle_kappa.reshape(ROWS, 128), solid_label.reshape(ROWS, 128), tile_active.reshape(1, 2),
    ]
    args = [pltpu.with_memory_space_constraint(a, pltpu.HBM) for a in args]
    hbm, vmem = pl.BlockSpec(memory_space=pltpu.HBM), pl.BlockSpec(memory_space=pltpu.VMEM)
    kept = [
        pltpu.VMEM(shape, F32)
        for shape in (
            (7, ROWS + 32, 128), (7, ROWS, 128), (7, ROWS + 16, 128), (6, ROWS, 128),
            (3, LAYERS, 128), (12, 8, 128), (2, 8, 128),
        )
    ]
    messages = [pltpu.VMEM((n, 128), F32) for n in PARTS]
    held = pl.pallas_call(
        functools.partial(exchange, nz),
        out_shape=kept,
        in_specs=[hbm] * 6,
        out_specs=[vmem] * 7,
        scratch_shapes=[
            pltpu.VMEM((7, ROWS, 128), jnp.bfloat16),
            pltpu.VMEM((7, ROWS, 128), jnp.bfloat16),
            pltpu.VMEM((3, ROWS, 128), jnp.bfloat16),
            pltpu.VMEM((ROWS, 128), F32),
            pltpu.VMEM((ROWS, 128), jnp.int32),
            pltpu.SMEM((1, 2), jnp.int32),
            pltpu.VMEM((3, ROWS, 128), F32),
            pltpu.VMEM((5, ROWS, 128), F32),
            pltpu.VMEM((2, ROWS, 128), F32),
            pltpu.VMEM((7, 8, 128), F32),
            *messages,
            *messages,
            pltpu.SemaphoreType.DMA((6,)),
            pltpu.SemaphoreType.DMA((9,)),
            pltpu.SemaphoreType.DMA((9,)),
            pltpu.SemaphoreType.REGULAR,
        ],
        compiler_params=pltpu.CompilerParams(
            collective_id=0, has_side_effects=True, vmem_limit_bytes=24 * 2**20
        ),
        name="exchange",
    )(*args)
    first, gradient = pl.pallas_call(
        finish,
        out_shape=[
            jax.ShapeDtypeStruct((7, 2, 256, 128), F32),
            jax.ShapeDtypeStruct((2, 256, 128), F32),
        ],
        in_specs=[vmem] * 7,
        out_specs=[hbm] * 2,
        scratch_shapes=[
            pltpu.VMEM((7, ROWS + 16, 128), F32),
            pltpu.VMEM((ROWS, 128), F32),
            pltpu.VMEM((7, 2, 256, 128), F32),
            pltpu.VMEM((2, 256, 128), F32),
            pltpu.SemaphoreType.DMA((CHUNKS,)),
            pltpu.SemaphoreType.DMA((CHUNKS,)),
        ],
        compiler_params=pltpu.CompilerParams(vmem_limit_bytes=24 * 2**20),
        name="finish",
    )(*held)
    voxels = EDGE * EDGE * EDGE
    return first.reshape(7, 2, 1, 1, voxels), gradient.reshape(2, 1, 1, voxels)


def solution(mesh):
    spec, one = P(None, "gx", "gy", "gz", None), P("gx", "gy", "gz", None)
    return jax.shard_map(
        functools.partial(on_device, mesh.shape["gz"]),
        mesh=mesh,
        in_specs=(spec, spec, spec, one, one, P("gx", "gy", "gz")),
        out_specs=(spec, one),
        check_vma=False,
    )
```

time: 17.6 us -> 16.3 us (0.926)
  the two profiles are of different devices: /device:TPU:1 before, /device:TPU:4 now
where the time goes in v3:
time: 16.3 us; the launch traced here: 16.2 us
  Pallas kernels  15.5 us (95%)
  between operations  0.64 us (4%)
    pallas_call x1, Pallas kernels, on_device(): pl.pallas_call(functools.partial(exchange, nz), out_shape=kept, in_specs=...  13.1 us
    pallas_call x1, Pallas kernels, on_device(): pl.pallas_call(finish, out_shape=[jax.ShapeDtypeStruct((7, 2, 256, 128),...  2.46 us

profile of v3, /device:TPU:4, one launch (start us, length us, event | category | flops | bytes accessed | tf_op | source)
XLA Modules:
  0.0 16.2 jit_solution(8658864493019671389)
XLA Ops:
  0.6 13.1 %exchange.1 = (f32[7,544,128]{2,1,0:T(8,128)S(1)}, f32[7,512,128]{2,1,0:T(8,128)S(1)}, f32[7,528,128]{2,1,0:T(8,128)S(1)}, f32[6,512,128]{2,1,0:T(8,128)S(1)}, f...) custom-call(bf16[7,512,128]{2,1,0:T(8,128)(2,1)} %bitcast.20, ...), custom_call_target="tpu_custom_call" | custom-call | tf_op jit(solution)/shard_map/exchange/pallas_call | solution.py:495
  13.7 2.5 %finish.1 = (f32[7,2,256,128]{3,2,1,0:T(8,128)}, f32[2,256,128]{2,1,0:T(8,128)}) custom-call(f32[7,544,128]{2,1,0:T(8,128)S(1)} %get-tuple-element.11.tf, f32[7,512,128]{2,1,0:T(8,128)S(1)} %get-tuple-element.12.tg, f32[7,528,128]{2,1,0:T(8,128)S(1)} %get-tuple-element.13.po, f32[6,512,128]{2,1,0:T(8,128)S(1)} %get-tuple-element.14.co, ...), custom_call_target="tpu_custom_call" | custom-call | tf_op jit(solution)/shard_map/finish/pallas_call | solution.py:523

commit v4 on v3

--- a/solution.py
+++ b/solution.py
@@ -126,7 +126,7 @@
     i_e, p_e = 31 * ox, ox
     sgx, sgy = (1 - 2 * gx).astype(F32), (1 - 2 * gy).astype(F32)
     first_x, first_y = gx == 0, gy == 0
-    fx, fy, bx, by = 1 + ox, 3 + oy, 1 + gx, 3 + gy
+    fx, fy = 1 + ox, 3 + oy
     zsign = jnp.where(kz == 0, -0.5, 0.5)
 
     @pl.when(gz == nz - 1)
@@ -149,6 +149,46 @@
         tf[n, pl.ds(16 * 33 + 1, 8, stride=2), :] = zero
         po[n, 0:8, :] = zero
         po[n, ROWS + 8 : ROWS + 16, :] = zero
+    def pack_y(read):
+        out = []
+        for h in range(2):
+            v = zero
+            for g in range(4):
+                rows = read(32 * h + 8 * g, h, 8 * g)
+                v = jnp.where(grp == g, pltpu.roll(rows, lax.rem(32 * (g - g_e) + 128, 128), 1), v)
+            out.append(v)
+        return out
+
+    def every8(ref, n):
+        return lambda x, h, i: ref[n, pl.ds(8 * x + s_e, 8, stride=8), :]
+
+
+    own_face_y = pack_y(lambda x, h, i: tf[fy, pl.ds(16 * (i + 1) + h + 2 * s_e, 8, stride=16), :])
+
+    def gather(n, first, count):
+        for p in range(2):
+            low, high = zp[4 * n + 2 * p], zp[4 * n + 2 * p + 1]
+            for k in range(count):
+                i = first + k
+                v = pltpu.roll(zm[n, tile8(256 * p + 8 * i), :], i, 1)
+                low = jnp.where(kz == i, v, low)
+                high = jnp.where(kz == ((i + 31) & 31), v, high)
+            zp[4 * n + 2 * p], zp[4 * n + 2 * p + 1] = low, high
+
+    zp[4:20] = jnp.zeros((16, 8, 128), F32)
+    faces = [zero] * 4
+    for i in range(32):
+        for p in range(2):
+            at = pl.ds(16 * (i + 1) + p, 8, stride=2)
+            v = jnp.where(kz == 0, tf[5, at, :], tf[6, at, :])
+            zm[0, 256 * p + 8 * i : 256 * p + 8 * i + 8, :] = v
+            v = pltpu.roll(v, i, 1)
+            faces[2 * p] = jnp.where(kz == i, v, faces[2 * p])
+            faces[2 * p + 1] = jnp.where(kz == (i + 31) % 32, v, faces[2 * p + 1])
+    for v in range(2):
+        s3[part(v)] = faces[2 * v]
+        s2[part(v)] = pltpu.roll(faces[2 * v + 1], 97, 1)
+    zy = pack_y(every8(zm, 0))
     loads[2].wait()
     for n in range(3):
         tv[n] = velb[n].astype(F32)
@@ -180,76 +220,68 @@
         d = [jnp.where(solid, 0.0, tv[n, pl.ds(16 * i + p, 8, stride=2), :]) for n in range(3)]
         return near, q, solid, rate, ar, b, d, ar * weighted(q, d)
 
+    def weights(i, p, ar):
+        g = [tg[n, pl.ds(16 * i + p, 8, stride=2), :] for n in range(7)]
+        return g, ar * (((g[0] + g[1]) + (g[2] + g[3])) + ((g[4] + g[5]) + g[6]))
+
     def layer(i, p, a):
         x = 32 * p + i
         near, q, solid, rate, ar, b, d, ars = cell(i, p, a)
         here = tile8(8 * x)
-        padded = tile8(8 * x + 8)
         for n, c in enumerate((ar, b, d[0], d[1], d[2])):
             co[n, here, :] = c
-        co[5, here, :] = jnp.where(solid, -4.0 * a * rate * rate, 0.0)
-        g = [tg[n, pl.ds(16 * i + p, 8, stride=2), :] for n in range(7)]
-        total = ((g[0] + g[1]) + (g[2] + g[3])) + ((g[4] + g[5]) + g[6])
-        w = ar * total
-        post = [b * g[0] + 0.25 * w]
-        for n in range(3):
-            even, odd = 0.125 * w, 0.5 * (w * d[n])
-            post.append(b * g[2 * n + 1] + (even + odd))
-            post.append(b * g[2 * n + 2] + (even - odd))
-        for n in range(7):
-            po[n, padded, :] = post[n]
+        g, w = weights(i, p, ar)
+        even = 0.125 * w
+        odd = 0.5 * (w * d[2])
+        post_5, post_6 = b * g[5] + (even + odd), b * g[6] + (even - odd)
         to_y = ar * (0.125 + 0.5 * sgy * d[1])
         bottom = kz == 0
-        zm[0, here, :] = jnp.where(bottom, near[3], near[4])
-        zm[1, here, :] = jnp.where(bottom, post[6], post[5])
+        zm[1, here, :] = jnp.where(bottom, post_6, post_5)
         zm[2, here, :] = ars + b * jnp.where(bottom, q[5], q[6])
         zm[3, here, :] = ar * (0.125 + zsign * d[2])
         zm[4, here, :] = jnp.where(sub == s_e, pick(first_y, near[2], near[1]), pltpu.roll(to_y, 4, 0))
         ym[0, here, :] = ars + b * pick(first_y, q[4], q[3])
         ym[1, here, :] = to_y
-        return near, q, ar, b, d, ars
-
-    def sweep(i, carry):
-        layer(i, 0, active[0])
-        layer(i, 1, active[1])
-        return carry
+        ym[2, here, :] = b * pick(first_y, g[3], g[4]) + (even + 0.5 * (w * (sgy * d[1])))
+        return near, q, ar, b, d, ars, g, w
 
     a_e = jnp.where(first_x, active[1], active[0])
-    near, q, ar, b, d, ars = layer(i_e, p_e, a_e)
+    near, q, ar, b, d, ars, g, w = layer(i_e, p_e, a_e)
     x_e = 63 * ox
     here_e = tile8(8 * x_e)
     to_x = ar * (0.125 + 0.5 * sgx * d[0])
     own_x = tf[fx, pl.ds(16 * (i_e + 1) + p_e, 8, stride=2), :]
     own_y = pick(first_y, near[2], near[1])
     s0[part(0)] = own_x
-    s0[part(1)] = po[bx, tile8(8 * x_e + 8), :]
+    s0[part(1)] = b * pick(first_x, g[1], g[2]) + (0.125 * w + 0.5 * (w * (sgx * d[0])))
     s0[part(2)] = ars + b * pick(first_x, q[2], q[1])
     s0[part(3)] = to_x
     s0[part(4)] = ym[1, here_e, :]
     s0[part(5)] = zm[3, here_e, :]
     pl.when(root)(copies[0].start)
 
-    lax.fori_loop(0, 32, sweep, 0, unroll=8)
-
-    def pack_y(read):
-        out = []
-        for h in range(2):
-            v = zero
-            for g in range(4):
-                rows = read(32 * h + 8 * g, h, 8 * g)
-                v = jnp.where(grp == g, pltpu.roll(rows, lax.rem(32 * (g - g_e) + 128, 128), 1), v)
-            out.append(v)
-        return out
-
-    def every8(ref, n, pad):
-        return lambda x, h, i: ref[n, pl.ds(8 * (x + pad) + s_e, 8, stride=8), :]
+    def block(first):
+        for k in range(8):
+            layer(first + k, 0, active[0])
+            layer(first + k, 1, active[1])
+
+    def sweep(c, carry):
+        for n in range(1, 5):
+            gather(n, 8 * c - 8, 8)
+        block(8 * c)
+        return carry
+
+    block(0)
+    lax.fori_loop(1, 4, sweep, 0)
+    for n in range(1, 5):
+        gather(n, 24, 8)
 
     packs = (
-        pack_y(lambda x, h, i: tf[fy, pl.ds(16 * (i + 1) + h + 2 * s_e, 8, stride=16), :]),
-        pack_y(every8(po, by, 1)),
-        pack_y(every8(ym, 0, 0)),
-        pack_y(every8(ym, 1, 0)),
-        pack_y(every8(zm, 3, 0)),
+        own_face_y,
+        pack_y(every8(ym, 2)),
+        pack_y(every8(ym, 0)),
+        pack_y(every8(ym, 1)),
+        pack_y(every8(zm, 3)),
     )
     for n, pair in enumerate(packs[:4]):
         s1[part(2 * n)] = pair[0]
@@ -262,38 +294,27 @@
     zp[0] = shifted(to_x, 32 * (3 * ox - g_e))
     s1[72:73, :] = zp[0, pl.ds(s_e, 1), :]
 
-    for n in range(5):
-
-        b0, t0, b1, t1 = (zero,) * 4
-        for i in range(32):
-            v0 = pltpu.roll(zm[n, 8 * i : 8 * i + 8, :], i, 1)
-            v1 = pltpu.roll(zm[n, 256 + 8 * i : 264 + 8 * i, :], i, 1)
-            bottom, top = kz == i, kz == (i + 31) % 32
-            b0, t0 = jnp.where(bottom, v0, b0), jnp.where(top, v0, t0)
-            b1, t1 = jnp.where(bottom, v1, b1), jnp.where(top, v1, t1)
-        t0, t1 = pltpu.roll(t0, 97, 1), pltpu.roll(t1, 97, 1)
-        if n < 4:
-            for msg, v, value in ((s3, 0, b0), (s3, 1, b1), (s2, 0, t0), (s2, 1, t1)):
-                msg[part(2 * n + v)] = value
-        else:
-            for v, line in enumerate((b0, b1, t0, t1)):
-                zp[1 + v] = line
-            for v, (msg, other_msg) in enumerate(((s3, s8), (s2, s7))):
-                for h in range(2):
-                    msg[72 + h : 73 + h, :] = zp[1 + 2 * v + h, pl.ds(s_c, 1), :]
-                    other_msg[8 + h : 9 + h, :] = zp[1 + 2 * v + h, pl.ds(s_e, 1), :]
+    for n in range(1, 4):
+        for k, (msg, v) in enumerate(((s3, 0), (s2, 0), (s3, 1), (s2, 1))):
+            packed = zp[4 * n + k]
+            msg[part(2 * n + v)] = packed if k % 2 == 0 else pltpu.roll(packed, 97, 1)
+    for v in range(2):
+        zp[21 + v] = pltpu.roll(zp[17 + 2 * v], 97, 1)
+    for msg, other_msg, base, step in ((s3, s8, 16, 2), (s2, s7, 21, 1)):
+        for h in range(2):
+            msg[72 + h : 73 + h, :] = zp[base + step * h, pl.ds(s_c, 1), :]
+            other_msg[8 + h : 9 + h, :] = zp[base + step * h, pl.ds(s_e, 1), :]
     s3[part(8)] = shifted(to_x, i_e)
     s2[part(8)] = shifted(to_x, i_e - 31)
 
     s_o, g_o = 7 * gy, 3 * gy
-    zp[5] = jnp.where(grp == g_o, shifted(own_y, 32 * (g_o - g_e)), 0.0)
-    zp[6] = jnp.where(grp == 3 * gx, shifted(own_x, 32 * (3 * gx - g_e)), 0.0)
-    s4[0:1, :] = zp[5, pl.ds(s_e, 1), :]
-    s4[1:2, :] = zp[6, pl.ds(s_e, 1), :]
+    zp[1] = jnp.where(grp == g_o, shifted(own_y, 32 * (g_o - g_e)), 0.0)
+    zp[2] = jnp.where(grp == 3 * gx, shifted(own_x, 32 * (3 * gx - g_e)), 0.0)
+    s4[0:1, :] = zp[1, pl.ds(s_e, 1), :]
+    s4[1:2, :] = zp[2, pl.ds(s_e, 1), :]
     z_e = zm[0, here_e, :]
     s6[...] = jnp.where(kz == 16, pltpu.roll(own_x, 16, 1), pltpu.roll(z_e, 31, 1))
     s5[...] = jnp.where(kz == 16, pltpu.roll(own_x, 113, 1), pltpu.roll(z_e, 97, 1))
-    zy = pack_y(every8(zm, 0, 0))
     s8[0:8, :] = jnp.where(kz == 7, pltpu.roll(zy[1], 39, 1), pltpu.roll(zy[0], 31, 1))
     s7[0:8, :] = jnp.where(kz == 8, pltpu.roll(zy[1], 105, 1), pltpu.roll(zy[0], 97, 1))
 
@@ -315,6 +336,29 @@
         pl.semaphore_wait(ready, 1)
         for k in order:
             pl.when(to_root[k])(copies[k].start)
+
+    def rest(i, p):
+        x = 32 * p + i
+        here = tile8(8 * x)
+        padded = tile8(8 * x + 8)
+        ar, b = co[0, here, :], co[1, here, :]
+        solid = solb[here, :] > 0
+        co[5, here, :] = jnp.where(solid, -4.0 * ar * ar, 0.0)
+        g, w = weights(i, p, ar)
+        po[0, padded, :] = b * g[0] + 0.25 * w
+        even = 0.125 * w
+        for n in range(3):
+            odd = 0.5 * (w * co[2 + n, here, :])
+            po[2 * n + 1, padded, :] = b * g[2 * n + 1] + (even + odd)
+            po[2 * n + 2, padded, :] = b * g[2 * n + 2] + (even - odd)
+
+    def finish_rest(c, carry):
+        for k in range(8):
+            rest(8 * c + k, 0)
+            rest(8 * c + k, 1)
+        return carry
+
+    lax.fori_loop(0, 4, finish_rest, 0)
 
     def arrival(k):
         return pltpu.make_async_remote_copy(
@@ -506,8 +550,8 @@
             pltpu.SMEM((1, 2), jnp.int32),
             pltpu.VMEM((3, ROWS, 128), F32),
             pltpu.VMEM((5, ROWS, 128), F32),
-            pltpu.VMEM((2, ROWS, 128), F32),
-            pltpu.VMEM((7, 8, 128), F32),
+            pltpu.VMEM((3, ROWS, 128), F32),
+            pltpu.VMEM((23, 8, 128), F32),
             *messages,
             *messages,
             pltpu.SemaphoreType.DMA((6,)),

time: 16.3 us -> 15.9 us (0.975)
  Pallas kernels: 15.5 us -> 15.1 us
    pallas_call x1, Pallas kernels: 13.1 us -> 12.6 us  [on_device(): pl.pallas_call(functools.partial(exchange, nz), out_shape=kept, in_specs=...]
where the time goes in v4:
time: 15.9 us; the launch traced here: 15.7 us
  Pallas kernels  15.1 us (95%)
  between operations  0.64 us (4%)
    pallas_call x1, Pallas kernels, on_device(): pl.pallas_call(functools.partial(exchange, nz), out_shape=kept, in_specs=...  12.6 us
    pallas_call x1, Pallas kernels, on_device(): pl.pallas_call(finish, out_shape=[jax.ShapeDtypeStruct((7, 2, 256, 128),...  2.46 us

profile of v4, /device:TPU:4, one launch (start us, length us, event | category | flops | bytes accessed | tf_op | source)
XLA Modules:
  0.0 15.7 jit_solution(17787117093150505602)
XLA Ops:
  0.6 12.6 %exchange.1 = (f32[7,544,128]{2,1,0:T(8,128)S(1)}, f32[7,512,128]{2,1,0:T(8,128)S(1)}, f32[7,528,128]{2,1,0:T(8,128)S(1)}, f32[6,512,128]{2,1,0:T(8,128)S(1)}, f...) custom-call(bf16[7,512,128]{2,1,0:T(8,128)(2,1)} %bitcast.20, ...), custom_call_target="tpu_custom_call" | custom-call | tf_op jit(solution)/shard_map/exchange/pallas_call | solution.py:539
  13.3 2.5 %finish.1 = (f32[7,2,256,128]{3,2,1,0:T(8,128)}, f32[2,256,128]{2,1,0:T(8,128)}) custom-call(f32[7,544,128]{2,1,0:T(8,128)S(1)} %get-tuple-element.11.tf, f32[7,512,128]{2,1,0:T(8,128)S(1)} %get-tuple-element.12.tg, f32[7,528,128]{2,1,0:T(8,128)S(1)} %get-tuple-element.13.po, f32[6,512,128]{2,1,0:T(8,128)S(1)} %get-tuple-element.14.co, ...), custom_call_target="tpu_custom_call" | custom-call | tf_op jit(solution)/shard_map/finish/pallas_call | solution.py:567
